TPU v7x, 128 devices: a whole 4x4x4 slice. The times are simulated.
128 devices in a mesh: tile: 16 (over y, x), depth: 8 (over z, core).
Axes of the slice: x: 4, y: 4, z: 4, core: 2. Of those that a mesh axis runs over, the one named last changes fastest.
Arguments:
- velocity: bfloat16 [3, 128, 1024, 1024], P(None, 'depth', 'tile'), may hold values from -7.5 to 7.5
- palette: float32 [4, 32], replicated, may hold values from 0.02 to 1
- bin_table: int32 [17], replicated, may hold values from 0 to 31
- hot_ids: int32 [16, 4], P('tile'), may hold values from 0 to 127
- repeats: int32 [16, 4], P('tile'), may hold values from 1 to 3
Outputs:
- image_rgb: float32 [3, 1024, 1024], P(None, 'tile', 'depth')
- image_transmit: float32 [1024, 1024], P('tile', 'depth')
- inset_rgb: float32 [16, 4, 3, 64, 1024], P('tile', None, None, None, 'depth')
- inset_transmit: float32 [16, 4, 64, 1024], P('tile', None, None, 'depth')
Inputs may be any that keep to these rules, and one draw needn't show every extreme that they name: `hot_ids`: brick ids, tile times 8 plus depth slab.
All inputs are finite; a program needn't handle non-finite values.
Results may differ from a plain program's by a relative error of at most 0.005.
Values may be sent and summed in bfloat16 or wider, within the bound.
A program may use at most 256 MiB of HBM per device.

v0:
```python
import jax
import jax.numpy as jnp
from jax import lax
from jax.sharding import PartitionSpec as P

KNOTS = 17
PAL = 32
MAXREP = 3


COEF_ONE = 0.75
COEF_TWO = -0.15
COEF_THREE = 1.0 / 60.0


def extended(array, sides, width):
    for axis, dim in sides:
        count, length = (lax.axis_size(axis), array.shape[dim])
        up = [(i, (i + 1) % count) for i in range(count)]
        down = [(j, i) for i, j in up]
        last = lax.slice_in_dim(array, length - width, length, axis=dim)
        initial = lax.slice_in_dim(array, 0, width, axis=dim)
        before = lax.ppermute(last, axis, up)
        after = lax.ppermute(initial, axis, down)
        array = jnp.concatenate([before, array, after], axis=dim)
    return array


def diff_roll(field, axis):
    first = jnp.roll(field, -1, axis) - jnp.roll(field, 1, axis)
    second = jnp.roll(field, -2, axis) - jnp.roll(field, 2, axis)
    third = jnp.roll(field, -3, axis) - jnp.roll(field, 3, axis)
    return COEF_ONE * first + COEF_TWO * second + COEF_THREE * third


def diff_pad(field, axis, count):

    def piece(offset):
        return lax.slice_in_dim(field, 3 + offset, 3 + offset + count, axis=axis).astype(
            jnp.float32
        )

    first = piece(1) - piece(-1)
    second = piece(2) - piece(-2)
    third = piece(3) - piece(-3)
    return COEF_ONE * first + COEF_TWO * second + COEF_THREE * third


def q_value(grads):
    total = grads[0][0] * grads[0][0] + grads[1][1] * grads[1][1] + grads[2][2] * grads[2][2]
    cross = grads[0][1] * grads[1][0] + grads[0][2] * grads[2][0] + grads[1][2] * grads[2][1]
    return -0.5 * (total + 2.0 * cross)


def shade(qfield, knot_vals):
    position = (jnp.tanh(qfield) + 1.0) * (0.5 * (KNOTS - 1))
    result = jnp.zeros((4,) + qfield.shape, jnp.float32)
    for knot in range(KNOTS):
        weight = jnp.maximum(0.0, 1.0 - jnp.abs(position - knot))
        result = result + knot_vals[:, knot][:, None, None, None] * weight[None]
    return result


def over(front, back):
    return jnp.concatenate([front[:3] + front[3:4] * back[:3], front[3:4] * back[3:4]], axis=0)


def repeat_fold(image, count):
    colour = image[:3]
    trans = image[3]
    acc = jnp.zeros_like(colour)
    power = jnp.ones_like(trans)
    for turn in range(MAXREP):
        live = turn < count
        acc = acc + jnp.where(live, power[None] * colour, 0.0)
        power = jnp.where(live, power * trans, power)
    return (acc, power)


def body(velocity, palette, bin_table, hot_ids, repeats):
    depth_cells = velocity.shape[1]
    width = velocity.shape[2]
    depth_total = depth_cells * lax.axis_size("depth")
    padded = extended(velocity, (("tile", 2), ("depth", 1)), 3)
    grads = []
    for comp in range(3):
        field = padded[comp]
        along_depth = diff_pad(field[:, 3 : 3 + width, :], 0, depth_cells)
        along_first = diff_pad(field[3 : 3 + depth_cells], 1, width)
        core = field[3 : 3 + depth_cells, 3 : 3 + width].astype(jnp.float32)
        grads.append([along_depth, along_first, diff_roll(core, 2)])
    qfield = q_value(grads)
    onehot = (bin_table[None, :] == jnp.arange(PAL, dtype=jnp.int32)[:, None]).astype(jnp.float32)
    knot_vals = jnp.dot(palette, onehot, precision=lax.Precision.HIGHEST)
    rgba = shade(qfield, knot_vals)
    tau = rgba[3] * (4.0 / depth_total)
    cum = jnp.cumsum(tau, axis=0)
    weight = (1.0 - jnp.exp(-tau)) * jnp.exp(-(cum - tau))
    colour = jnp.sum(rgba[:3] * weight[None], axis=1)
    slab_image = jnp.concatenate([colour, jnp.exp(-cum[-1])[None]], axis=0)
    count_depth = lax.axis_size("depth")
    columns = slab_image.shape[2] // count_depth
    every_slab = lax.all_gather(slab_image[None], "depth", axis=0, tiled=True)
    slabs = lax.dynamic_slice_in_dim(every_slab, lax.axis_index("depth") * columns, columns, 3)

    def fold_step(carry, image):
        return (over(carry, image), None)

    start_image = jnp.concatenate(
        [jnp.zeros((3, width, columns), jnp.float32), jnp.ones((1, width, columns), jnp.float32)],
        axis=0,
    )
    once, _ = lax.scan(fold_step, start_image, slabs)
    twice = over(once, once)
    stored = slabs.astype(jnp.bfloat16)
    wanted = hot_ids[0]
    counts = repeats[0]
    every_brick = lax.all_gather(stored, "tile", axis=0, tiled=True)
    chosen = jnp.take(every_brick, wanted, axis=0).astype(jnp.float32)
    inset_colour, inset_trans = jax.vmap(repeat_fold)(chosen, counts)
    return (twice[:3], twice[3], inset_colour[None], inset_trans[None])


def solution(mesh):
    placed = (P(None, "depth", "tile", None), P(), P(), P("tile", None), P("tile", None))
    return jax.shard_map(
        body,
        mesh=mesh,
        in_specs=placed,
        out_specs=(
            P(None, "tile", "depth"),
            P("tile", "depth"),
            P("tile", None, None, None, "depth"),
            P("tile", None, None, "depth"),
        ),
        check_vma=False,
    )
```

profile of v0, /device:TPU:0, one launch (start us, length us, event | category | flops | bytes accessed | tf_op | source)
XLA Modules:
  0.0 376.2 jit_solution(2098384608166940151)
XLA Ops:
  7.2 0.0 copy-start
  7.2 0.0 all-gather.6.cloned.1.call-start
  7.2 1.7 fusion.45
  8.9 0.1 copy.13
  9.1 1.6 collective-permute-start
  10.7 0.1 copy.14
  10.8 3.8 %collective-permute-start.1 = (bf16[3,16,3,1024]{3,1,2,0:T(8,128)(2,1)S(1)}, bf16[3,16,3,1024]{3,1,2,0:T(8,128)(2,1)S(1)}, u32[]{:S(2)}, u32[]{:S(2)}) collective-permute-start(bf16[3,16,3,1024]{3,1,2,0:T(8,128)(2,1)S(1)} %copy.14), channel_id=1, source_target_pairs={{8,0},{16,8},{24,16},{32,24},{40,32},{48,40},{56,48},{64,56},{72,6... | collective-permute-start | bytes 884744 | tf_op jit(solution)/shard_map/ppermute | solution.py:24
  14.7 6.8 %collective-permute-done = bf16[3,16,3,1024]{3,1,2,0:T(8,128)(2,1)S(1)} collective-permute-done((bf16[3,16,3,1024]{3,1,2,0:T(8,128)(2,1)S(1)}, bf16[3,16,3,1024]{3,1,2,0:T(8,128)(2,1)S(1)}, u32[]{:S(2)}, u32[]{:S(2)}) %collective-permute-start) | collective-permute-done | bytes 294944 | tf_op jit(solution)/shard_map/ppermute | solution.py:23
  21.4 0.3 copy.11
  21.7 0.3 copy.12
  22.0 0.0 slice-start.1
  22.0 3.2 pad_maximum_fusion.4
  25.2 0.0 collective-permute-start.2
  25.3 2.9 collective-permute-start.3
  28.2 0.1 convolution_bitcast_fusion
  28.3 0.4 slice_reduce_fusion.16
  28.8 3.4 pad_maximum_fusion.2
  32.2 3.1 slice_bitcast_fusion.6
  35.3 8.4 %collective-permute-done.2 = bf16[3,3,70,1024]{3,2,1,0:T(8,128)(2,1)S(1)} collective-permute-done((bf16[3,3,70,1024]{3,2,1,0:T(8,128)(2,1)S(1)}, bf16[3,3,70,1024]{3,2,1,0:T(8,128)(2,1)S(1)}, u32[]{:S(2)}, u32[]{:S(2)}) %collective-permute-start.2) | collective-permute-done | bytes 1290272 | tf_op jit(solution)/shard_map/ppermute | solution.py:23
  43.7 6.3 %pad_maximum_fusion.1 = bf16[3,22,70,1024]{3,2,1,0:T(8,128)(2,1)} fusion(bf16[3,3,70,1024]{3,2,1,0:T(8,128)(2,1)S(1)} %collective-permute-done.3, bf16[3,16,3,1024]{3,2,1,0:T(4,128)(2,1)S(1)} %copy.12, bf16[3,16,64,1024]{3,2,1,0:T(8,128)(2,1)S(1)} %bitcast.72, bf16[3,16,3,1024]{3,2,1,0:T(4,128)(2,1)S(1)} %copy.11, ...), kind=kLoop, calls=%fused_computation.11 | loop fusion | flops 47308800 | bytes 18923520 | tf_op jit(solution)/shard_map/concatenate | solution.py:25
  50.0 4.5 %slice_bitcast_fusion.3 = (bf16[22,70,1024]{2,1,0:T(8,128)(2,1)S(1)}, bf16[22,70,1024]{2,1,0:T(8,128)(2,1)S(1)}, bf16[22,70,1024]{2,1,0:T(8,128)(2,1)S(1)}) fusion(bf16[3,22,70,1024]{3,2,1,0:T(8,128)(2,1)} %pad_maximum_fusion.1), kind=kLoop, calls=%fused_computation.76 | loop fusion | bytes 18923520 | tf_op jit(solution)/shard_map/squeeze | solution.py:87
  54.5 1.3 slice_convert_fusion
  55.8 4.6 %fusion.58 = (f32[16,64,1023]{2,1,0:T(8,128)}, f32[16,64,1023]{2,1,0:T(8,128)}) fusion(f32[16,64,1024]{2,1,0:T(8,128)S(1)} %get-tuple-element.120), kind=kLoop, calls=%fused_computation.143 | loop fusion | bytes 16760832 | tf_op jit(solution)/shard_map/jit(_roll_static)/slice | solution.py:30
  60.4 4.6 %fusion.60 = (f32[16,64,1022]{2,1,0:T(8,128)}, f32[16,64,1022]{2,1,0:T(8,128)}) fusion(f32[16,64,1024]{2,1,0:T(8,128)S(1)} %get-tuple-element.120), kind=kLoop, calls=%fused_computation.145 | loop fusion | bytes 16744448 | tf_op jit(solution)/shard_map/jit(_roll_static)/slice | solution.py:31
  65.0 4.6 %fusion.62 = (f32[16,64,1021]{2,1,0:T(8,128)}, f32[16,64,1021]{2,1,0:T(8,128)}) fusion(f32[16,64,1024]{2,1,0:T(8,128)S(1)} %get-tuple-element.120), kind=kLoop, calls=%fused_computation.147 | loop fusion | bytes 16728064 | tf_op jit(solution)/shard_map/jit(_roll_static)/slice | solution.py:32
  69.6 4.6 %fusion.52 = (f32[16,64,1023]{2,1,0:T(8,128)}, f32[16,64,1023]{2,1,0:T(8,128)}) fusion(f32[16,64,1024]{2,1,0:T(8,128)S(1)} %get-tuple-element.121), kind=kLoop, calls=%fused_computation.137 | loop fusion | bytes 16760832 | tf_op jit(solution)/shard_map/jit(_roll_static)/slice | solution.py:30
  74.2 4.6 %fusion.54 = (f32[16,64,1022]{2,1,0:T(8,128)}, f32[16,64,1022]{2,1,0:T(8,128)}) fusion(f32[16,64,1024]{2,1,0:T(8,128)S(1)} %get-tuple-element.121), kind=kLoop, calls=%fused_computation.139 | loop fusion | bytes 16744448 | tf_op jit(solution)/shard_map/jit(_roll_static)/slice | solution.py:31
  78.8 4.6 %fusion.56 = (f32[16,64,1021]{2,1,0:T(8,128)}, f32[16,64,1021]{2,1,0:T(8,128)}) fusion(f32[16,64,1024]{2,1,0:T(8,128)S(1)} %get-tuple-element.121), kind=kLoop, calls=%fused_computation.141 | loop fusion | bytes 16728064 | tf_op jit(solution)/shard_map/jit(_roll_static)/slice | solution.py:32
  83.4 0.2 fusion.57
  83.6 1.0 fusion.59
  84.6 1.2 fusion.61
  85.8 1.1 fusion.63
  87.0 1.2 fusion.53
  88.1 1.1 fusion.55
  89.3 0.6 slice_convert_fusion.2
  89.9 4.9 %fusion.46 = (f32[16,64,1023]{2,1,0:T(8,128)}, f32[16,64,1023]{2,1,0:T(8,128)}) fusion(f32[16,64,1024]{2,1,0:T(8,128)S(1)} %slice_convert_fusion.2), kind=kLoop, calls=%fused_computation.131 | loop fusion | bytes 16760832 | tf_op jit(solution)/shard_map/jit(_roll_static)/slice | solution.py:30
  94.8 4.6 %fusion.48 = (f32[16,64,1022]{2,1,0:T(8,128)}, f32[16,64,1022]{2,1,0:T(8,128)}) fusion(f32[16,64,1024]{2,1,0:T(8,128)S(1)} %slice_convert_fusion.2), kind=kLoop, calls=%fused_computation.133 | loop fusion | bytes 16744448 | tf_op jit(solution)/shard_map/jit(_roll_static)/slice | solution.py:31
  99.4 4.6 %fusion.50 = (f32[16,64,1021]{2,1,0:T(8,128)}, f32[16,64,1021]{2,1,0:T(8,128)}) fusion(f32[16,64,1024]{2,1,0:T(8,128)S(1)} %slice_convert_fusion.2), kind=kLoop, calls=%fused_computation.135 | loop fusion | bytes 16728064 | tf_op jit(solution)/shard_map/jit(_roll_static)/slice | solution.py:32
  104.0 1.1 fusion.47
  105.1 1.2 fusion.49
  106.3 1.2 fusion.51
  107.6 63.0 %subtract_maximum_fusion.16 = (f32[16,64,1024]{2,1,0:T(8,128)}, f32[16,64,1024]{2,1,0:T(8,128)}) fusion(bf16[16,70,1024]{2,1,0:T(8,128)(2,1)} %get-tuple-element.55, f32[16,64,1021]{2,1,0:T(8,128)} %get-tuple-element.110, f32[16,64,3]{2,1,0:T(8,128)} %get-tuple-element.112, f32[16,64,3]{2,1,0:T(8,128)} %get-tuple-element.111, ...), kind=kLoop, calls=%fused_computation.73 | loop fusion | flops 150994944 | bytes 159383552 | tf_op jit(solution)/shard_map/max | solution.py:59
  170.6 23.4 %subtract_maximum_fusion.15 = (f32[16,64,1024]{2,1,0:T(8,128)}, f32[16,64,1024]{2,1,0:T(8,128)}, f32[16,64,1024]{2,1,0:T(8,128)}, f32[16,64,1024]{2,1,0:T(8,128)...) fusion(f32[16,64,1024]{2,1,0:T(8,128)} %get-tuple-element.48), kind=kLoop, calls=%fused_computation.72 | loop fusion | flops 67108864 | bytes 71303168 | tf_op jit(solution)/shard_map/max | solution.py:59
  194.0 27.8 %multiply_add_fusion = f32[4,16,64,1024]{3,2,1,0:T(8,128)S(1)} fusion(f32[16,64,1024]{2,1,0:T(8,128)} %get-tuple-element.76, f32[4]{0:T(128)S(1)} %get-tuple-element.23, f32[16,64,1024]{2,1,0:T(8,128)} %get-tuple-element.62, f32[4]{0:T(128)S(1)} %get-tuple-element.24, f32[16,64,1024]{2,1,0:T(8,128)} %get-tuple-element.63, f32[4]{0:T(128)S(1)} %get-tuple-element.25, ...), kind=kLoop, calls=%fused_computation.8 | loop fusion | flops 138412032 | bytes 88080656 | tf_op jit(solution)/shard_map/add | solution.py:60
  221.9 0.7 fusion.35
  222.6 5.0 %copy-done.2 = f32[4,16,64,1024]{3,2,1,0:T(8,128)} copy-done((f32[4,16,64,1024]{3,2,1,0:T(8,128)}, f32[4,16,64,1024]{3,2,1,0:T(8,128)S(1)}, u32[]{:S(2)}) %copy-start.2) | copy-done | bytes 16777240
  227.6 1.2 fusion.34
  228.8 0.7 fusion.38
  229.6 6.3 %fusion.3 = f32[3,64,1024]{2,1,0:T(8,128)S(1)} fusion(f32[4,16,64,1024]{3,2,1,0:T(8,128)} %copy-done.2, f32[16,64,1024]{2,1,0:T(8,128)S(1)} %fusion.34), kind=kLoop, calls=%fused_computation.10 | loop fusion | flops 6094848 | bytes 17563648 | tf_op jit(solution)/shard_map/reduce_sum | solution.py:99
  235.9 2.2 pad_maximum_fusion.5
  238.1 0.0 all-gather.6.cloned.1.call-update
  238.1 0.0 all-gather.4.cloned.1.call-start
  238.2 51.8 %all-gather.6.cloned.1.call-done = f32[32,64,1024]{2,1,0:T(8,128)} async-done(((f32[4,64,1024]{2,1,0:T(8,128)}), f32[32,64,1024]{2,1,0:T(8,128)}) %all-gather.6.cloned.1.call-update) | async-done | bytes 8388624 | tf_op jit(solution)/shard_map/all_gather | solution.py:103
  290.0 2.3 fusion.43
  292.2 0.0 all-gather.4.cloned.1.call-update
  292.3 0.7 while.10
  293.0 0.6 multiply_bitcast_fusion
  293.6 0.7 multiply_add_fusion.1
  294.3 68.8 %all-gather.4.cloned.1.call-done = bf16[128,4,64,128]{3,2,1,0:T(8,128)(2,1)} async-done(((bf16[8,4,64,128]{3,2,1,0:T(8,128)(2,1)}), bf16[128,4,64,128]{3,2,1,0:T(8,128)(2,1)}) %all-gather.4.cloned.1.call-update) | async-done | bytes 8388624 | tf_op jit(solution)/shard_map/all_gather | solution.py:118
  363.0 4.0 %gather_fusion = bf16[4,4,64,128]{3,2,1,0:T(8,128)(2,1)S(1)} fusion(bf16[128,4,64,128]{3,2,1,0:T(8,128)(2,1)} %all-gather.4.cloned.1.call-done, s32[1024]{0:T(1024)S(1)} %pad_clamp_fusion), kind=kCustom, calls=%fused_computation | custom fusion | bytes 524304 | tf_op jit(solution)/shard_map/jit(_take)/gather | solution.py:119
  367.0 0.1 select_convert_fusion
  367.1 0.1 select_bitcast_fusion
  367.2 0.8 multiply_select_fusion
  368.0 0.9 add_bitcast_fusion
  (48 shorter events, 0.4 us)
Async XLA Ops:
  7.2 21.0 %copy-start = (f32[4,32]{1,0:T(4,128)S(1)}, f32[4,32]{1,0:T(4,128)}, u32[]{:S(2)}) copy-start(f32[4,32]{1,0:T(4,128)} %param.8) | copy-start | bytes 1540
  7.2 282.8 %all-gather.6.cloned.1.call-start = ((), (), s32[]{:S(2)}) async-start(), calls=%async_computation.1 | async-start | bytes 9437184 | tf_op jit(solution)/shard_map/all_gather | solution.py:103
  9.1 12.4 %collective-permute-start = (bf16[3,16,3,1024]{3,1,2,0:T(8,128)(2,1)S(1)}, bf16[3,16,3,1024]{3,1,2,0:T(8,128)(2,1)S(1)}, u32[]{:S(2)}, u32[]{:S(2)}) collective-permute-start(bf16[3,16,3,1024]{3,1,2,0:T(8,128)(2,1)S(1)} %copy.13), channel_id=1, source_target_pairs={{0,8},{8,16},{16,24},{24,32},{32,40},{40,48},{48,56},{56,64},{64,7... | collective-permute-start | bytes 884744 | tf_op jit(solution)/shard_map/ppermute | solution.py:23
  10.7 18.1 %slice-start = ((s8[6291456]{0:T(1024)(128)(4,1)}), s8[4194304]{0:T(1024)(128)(4,1)S(1)}, s32[]{:S(2)}) async-start(s8[6291456]{0:T(1024)(128)(4,1)} %bitcast.71), calls=%async_computation.2 | async-start | bytes 8388608
  10.8 10.9 %collective-permute-start.1 = (bf16[3,16,3,1024]{3,1,2,0:T(8,128)(2,1)S(1)}, bf16[3,16,3,1024]{3,1,2,0:T(8,128)(2,1)S(1)}, u32[]{:S(2)}, u32[]{:S(2)}) collective-permute-start(bf16[3,16,3,1024]{3,1,2,0:T(8,128)(2,1)S(1)} %copy.14), channel_id=1, source_target_pairs={{8,0},{16,8},{24,16},{32,24},{40,32},{48,40},{56,48},{64,56},{72,6... | collective-permute-start | bytes 884744 | tf_op jit(solution)/shard_map/ppermute | solution.py:24
  22.0 6.2 %copy-start.5 = (s32[17]{0:T(128)S(1)}, s32[17]{0:T(128)}, u32[]{:S(2)}) copy-start(s32[17]{0:T(128)} %param.9) | copy-start | bytes 208
  22.0 6.8 %slice-start.1 = ((s8[6291456]{0:T(1024)(128)(4,1)}), s8[2097152]{0:T(1024)(128)(4,1)S(1)}, s32[]{:S(2)}) async-start(s8[6291456]{0:T(1024)(128)(4,1)} %bitcast.71), calls=%async_computation.3 | async-start | bytes 4194304
  25.2 18.4 %collective-permute-start.2 = (bf16[3,3,70,1024]{3,2,1,0:T(8,128)(2,1)S(1)}, bf16[3,3,70,1024]{3,2,1,0:T(8,128)(2,1)S(1)}, u32[]{:S(2)}, u32[]{:S(2)}) collective-permute-start(bf16[3,3,70,1024]{3,2,1,0:T(8,128)(2,1)S(1)} %get-tuple-element.57), channel_id=1, source_target_pairs={{0,1},{1,2},{2,3},{3,4},{4,5},{5,6},{6,7},{7,0},{8,9},{9,10},{10,1... | collective-permute-start | bytes 3870728 | tf_op jit(solution)/shard_map/ppermute | solution.py:23
  25.3 18.4 %collective-permute-start.3 = (bf16[3,3,70,1024]{3,2,1,0:T(8,128)(2,1)S(1)}, bf16[3,3,70,1024]{3,2,1,0:T(8,128)(2,1)S(1)}, u32[]{:S(2)}, u32[]{:S(2)}) collective-permute-start(bf16[3,3,70,1024]{3,2,1,0:T(8,128)(2,1)S(1)} %get-tuple-element.58), channel_id=1, source_target_pairs={{1,0},{2,1},{3,2},{4,3},{5,4},{6,5},{7,6},{0,7},{9,8},{10,9},{11,1... | collective-permute-start | bytes 3870728 | tf_op jit(solution)/shard_map/ppermute | solution.py:24
  170.6 23.5 %copy-start.3 = (f32[16,64,1024]{2,1,0:T(8,128)S(1)}, f32[16,64,1024]{2,1,0:T(8,128)}, u32[]{:S(2)}) copy-start(f32[16,64,1024]{2,1,0:T(8,128)} %get-tuple-element.47) | copy-start | bytes 12582916
  221.9 5.7 %copy-start.2 = (f32[4,16,64,1024]{3,2,1,0:T(8,128)}, f32[4,16,64,1024]{3,2,1,0:T(8,128)S(1)}, u32[]{:S(2)}) copy-start(f32[4,16,64,1024]{3,2,1,0:T(8,128)S(1)} %multiply_add_fusion) | copy-start | bytes 50331652
  235.9 56.4 %copy-start.7 = (s32[1,4]{1,0:T(1,128)S(1)}, s32[1,4]{1,0:T(1,128)}, u32[]{:S(2)}) copy-start(s32[1,4]{1,0:T(1,128)} %param.10) | copy-start | bytes 52
  235.9 56.4 %copy-start.6 = (s32[1,4]{1,0:T(1,128)S(1)}, s32[1,4]{1,0:T(1,128)}, u32[]{:S(2)}) copy-start(s32[1,4]{1,0:T(1,128)} %param.11) | copy-start | bytes 52
  235.9 56.4 %copy-start.4 = (f32[4,64,128]{2,1,0:T(8,128)S(1)}, f32[4,64,128]{2,1,0:T(8,128)}, u32[]{:S(2)}) copy-start(f32[4,64,128]{2,1,0:T(8,128)} %constant.41.clone.1) | copy-start | bytes 393220
  238.1 124.9 %all-gather.4.cloned.1.call-start = ((), (), s32[]{:S(2)}) async-start(), calls=%async_computation | async-start | bytes 8912896 | tf_op jit(solution)/shard_map/all_gather | solution.py:118
  289.9 78.9 %copy-start.1 = (f32[4,32]{1,0:T(4,128)S(1)}, f32[4,32]{1,0:T(4,128)}, u32[]{:S(2)}) copy-start(f32[4,32]{1,0:T(4,128)} %param.8) | copy-start | bytes 1540
Sparse Core Ops, SparseCore 0:
  238.2 51.6 all-gather.5
  292.4 70.6 all-gather.3
where the time goes:
time: 382 us; the launch traced here: 376 us
  other arithmetic  146 us (38%)
  waiting for transfers between devices  136 us (36%)
  local copies, waits for them, and re-layouts  70.6 us (18%)
  between operations  14.8 us (4%)
  starting transfers between devices  8.52 us (2%)
    max x2, other arithmetic, shade(): weight = jnp.maximum(0.0, 1.0 - jnp.abs(position - knot))  86.5 us
    all_gather x1, waiting for transfers between devices, body(): every_brick = lax.all_gather(stored, 'tile', axis=0, tiled=True)  68.8 us
    all_gather x1, waiting for transfers between devices, body(): every_slab = lax.all_gather(slab_image[None], 'depth', axis=0, tiled=True)  51.8 us
    add x1, other arithmetic, shade(): result = result + knot_vals[:, knot][:, None, None, None] * weight[None]  27.8 us
    slice x6, local copies, waits for them, and re-layouts, diff_roll(): first = jnp.roll(field, -1, axis) - jnp.roll(field, 1, axis)  17.4 us
    slice x6, local copies, waits for them, and re-layouts, diff_roll(): second = jnp.roll(field, -2, axis) - jnp.roll(field, 2, axis)  17.4 us
    slice x6, local copies, waits for them, and re-layouts, diff_roll(): third = jnp.roll(field, -3, axis) - jnp.roll(field, 3, axis)  16.3 us
    ppermute x2, waiting for transfers between devices, extended(): before = lax.ppermute(last, axis, up)  15.1 us
  transfers between devices with their start and end apart: 6, of which 4 were waited for; matrix products, arithmetic and copies ran while one was open for 2% of the time, Pallas kernels for 0%

commit v1 on v0

v1 whole, which is shorter than its diff:
```python
import functools
import math

import jax
import jax.numpy as jnp
import ml_dtypes
import numpy as np
from jax import lax
from jax.experimental import pallas as pl
from jax.experimental.pallas import tpu as pltpu
from jax.sharding import PartitionSpec as P

KNOTS = 17
MAXREP = 3
STENCIL = ((1, 45.0), (2, -9.0), (3, 1.0))
TAPS = tuple((k, c) for k, c in STENCIL) + tuple((-k, -c) for k, c in STENCIL)
Q_SCALE = -0.5 / 3600.0
BF = jnp.bfloat16
F32 = jnp.float32
ROWS = 16
WIDE = 256
AXIS = 4


def depth_matrix(cells):
    m = np.zeros((cells * ROWS, (cells + 6) * ROWS), np.float32)
    for z in range(cells):
        for r in range(ROWS):
            for k, c in TAPS:
                m[z * ROWS + r, (z + 3 + k) * ROWS + r] = c
    return m


def first_matrix(tiles):
    m = np.zeros((tiles, 4 * ROWS, 13 * ROWS), np.float32)
    for t in range(tiles):
        for p in range(4):
            for r in range(ROWS):
                for k, c in TAPS:
                    g = r + k
                    if 0 <= g < ROWS:
                        col = 4 * ROWS + p * ROWS + g
                    elif g < 0:
                        col = p * ROWS + ROWS + g if t > 0 else 12 * ROWS + 3 * p + 3 + g
                    else:
                        col = 8 * ROWS + p * ROWS + g - ROWS if t < tiles - 1 else 12 * ROWS + 3 * p + g - ROWS
                    m[t, p * ROWS + r, col] = c
    return m


def second_matrix():
    m = np.zeros((2 * WIDE, WIDE), np.float32)
    for l in range(WIDE):
        for k, c in TAPS:
            m[128 + l + k, l] = c
    return m


def pack_matrix():
    m = np.zeros((2, ROWS, 4 * ROWS), np.float32)
    for p in range(4):
        for r in range(3):
            m[0, 3 * p + r, p * ROWS + r] = 1.0
            m[1, 3 * p + r, p * ROWS + ROWS - 3 + r] = 1.0
    return m


def render_kernel(
    sizes,
    vel, palette, bins, hot_smem, hot_vmem, reps, dz_ref, dx_ref, band_ref, pack_ref,
    img_rgb, img_t, ins_rgb, ins_t,
    vz, xsend, xh, grad, tab, packets, arrive, held, shelf, picked, landed, hot_all, hot_here,
    own_sem, zs_sem, zr_sem, xs_sem, xr_sem, hs_sem, hr_sem, hl_sem,
    as_sem, ar_sem, s1_sem, r1_sem, s2_sem, r2_sem,
):
    cells, width, length, n_depth, n_tile, hot = sizes
    tiles = width // ROWS
    blocks = length // WIDE
    tile = lax.axis_index("tile")
    me = lax.axis_index("depth")
    pos = (tile // AXIS, lax.rem(tile, AXIS))

    def peer(axis, i):
        place = lax.rem(pos[axis] + i, AXIS)
        return place, (place * AXIS + pos[1] if axis == 0 else pos[0] * AXIS + place)

    tile_up = lax.rem(tile + 1, n_tile)
    tile_down = lax.rem(tile + n_tile - 1, n_tile)
    depth_up = lax.rem(me + 1, n_depth)
    depth_down = lax.rem(me + n_depth - 1, n_depth)

    def own_copy(t):
        rows = pl.ds(t * ROWS, ROWS)
        return pltpu.make_async_copy(
            vel.at[:, :, rows, :], vz.at[:, pl.ds(3, cells), rows, :], own_sem.at[t]
        )

    for t in (0, 3, 1, 2):
        own_copy(t).start()

    barrier = pltpu.get_barrier_semaphore()
    for t in (tile_up, tile_down):
        pl.semaphore_signal(barrier, inc=1, device_id={"tile": t})
    for i in range(1, n_depth):
        pl.semaphore_signal(barrier, inc=1, device_id={"depth": lax.rem(me + i, n_depth)})
    for axis in (0, 1):
        for i in range(1, AXIS):
            pl.semaphore_signal(barrier, inc=1, device_id={"tile": peer(axis, i)[1]})
    pl.semaphore_wait(barrier, 2 + n_depth - 1 + 2 * (AXIS - 1))

    def z_copy(s, up):
        rows = pl.ds(lax.rem(s + 1, tiles) * ROWS, ROWS)
        source, target = (cells - 3, 0) if up else (0, cells + 3)
        return pltpu.make_async_remote_copy(
            src_ref=vel.at[:, pl.ds(source, 3), rows, :],
            dst_ref=vz.at[:, pl.ds(target, 3), rows, :],
            send_sem=zs_sem.at[s, int(up)],
            recv_sem=zr_sem.at[s, int(up)],
            device_id={"depth": depth_up if up else depth_down},
        )

    for s in range(tiles):
        for up in (True, False):
            z_copy(s, up).start()

    def hot_copy(axis, i):
        return pltpu.make_async_remote_copy(
            src_ref=hot_vmem,
            dst_ref=hot_all.at[axis, pos[axis]],
            send_sem=hs_sem.at[axis, i - 1],
            recv_sem=hr_sem.at[axis, pos[axis]],
            device_id={"tile": peer(axis, i)[1]},
        )

    def hot_arrival(axis, i):
        place, to = peer(axis, i)
        return pltpu.make_async_remote_copy(
            src_ref=hot_vmem, dst_ref=hot_all.at[axis, place],
            send_sem=hs_sem.at[axis, i - 1], recv_sem=hr_sem.at[axis, place],
            device_id={"tile": to},
        )

    for axis in (0, 1):
        for i in range(1, AXIS):
            hot_copy(axis, i).start()
        hot_all[axis, pos[axis]] = hot_vmem[...]

    own_copy(0).wait()
    own_copy(3).wait()
    for side in (0, 1):
        rows = pl.ds((tiles - 1) * ROWS * side, ROWS)

        def pack(g, carry, side=side, rows=rows):
            planes = vz[g // (cells // 4), pl.ds(3 + 4 * lax.rem(g, cells // 4), 4), rows, :]
            xsend[side, g] = jnp.dot(
                pack_ref[side], planes.reshape(4 * ROWS, length), preferred_element_type=F32
            ).astype(BF)
            return carry

        lax.fori_loop(0, 3 * cells // 4, pack, 0)

    def x_copy(side):
        return pltpu.make_async_remote_copy(
            src_ref=xsend.at[side],
            dst_ref=xh.at[1 - side],
            send_sem=xs_sem.at[side],
            recv_sem=xr_sem.at[side],
            device_id={"tile": tile_up if side else tile_down},
        )

    x_copy(0).start()
    x_copy(1).start()
    xh[2] = jnp.zeros(xh.shape[1:], BF)

    lane = lax.broadcasted_iota(jnp.int32, (8, 128), 1)
    for c in range(4):
        scale = -4.0 / (cells * n_depth) * math.log2(math.e) if c == 3 else 1.0
        values = [palette[c, bins[k]] * scale for k in range(KNOTS)]
        base = jnp.full((8, 128), values[KNOTS - 1], F32)
        slope = jnp.zeros((8, 128), F32)
        for k in range(KNOTS - 1):
            base = jnp.where(lane == k, values[k], base)
            slope = jnp.where(lane == k, values[k + 1] - values[k], slope)
        tab[2 * c] = base
        tab[2 * c + 1] = slope

    own_copy(1).wait()
    own_copy(2).wait()

    def a2a_copy(s, to):
        return pltpu.make_async_remote_copy(
            src_ref=packets.at[s, to],
            dst_ref=arrive.at[s, me],
            send_sem=as_sem.at[s, to],
            recv_sem=ar_sem.at[s, me],
            device_id={"depth": to},
        )

    def a2a_arrival(s, source):
        return pltpu.make_async_remote_copy(
            src_ref=packets.at[s, source],
            dst_ref=arrive.at[s, source],
            send_sem=as_sem.at[s, source],
            recv_sem=ar_sem.at[s, source],
            device_id={"depth": source},
        )

    def a2a_own(s):
        return pltpu.make_async_copy(packets.at[s, me], arrive.at[s, me], ar_sem.at[s, me])

    def block_step(b, s):
        t = lax.rem(s + 1, tiles)
        row = pl.multiple_of(t * ROWS, ROWS)
        above = pl.multiple_of(jnp.maximum(t - 1, 0) * ROWS, ROWS)
        below = pl.multiple_of(jnp.minimum(t + 1, tiles - 1) * ROWS, ROWS)
        side = jnp.where(t == 0, 0, jnp.where(t == tiles - 1, 1, 2))
        col = pl.multiple_of(b * WIDE, WIDE)
        before = pl.multiple_of(lax.rem(col + length - 128, length), 128)
        after = pl.multiple_of(lax.rem(col + WIDE, length), 128)
        cols = pl.ds(col, WIDE)
        size = cells * ROWS
        for comp in range(3):
            column = vz[comp, :, pl.ds(row, ROWS), cols].reshape((cells + 6) * ROWS, WIDE)
            grad[3 * comp] = jnp.dot(dz_ref[...], column, preferred_element_type=F32)
            for quad in range(cells // 4):
                zs = pl.ds(3 + 4 * quad, 4)
                parts = [
                    vz[comp, zs, pl.ds(r, ROWS), cols].reshape(4 * ROWS, WIDE)
                    for r in (above, row, below)
                ] + [xh[side, comp * (cells // 4) + quad, :, cols]]
                grad[3 * comp + 1, pl.ds(quad * 4 * ROWS, 4 * ROWS)] = jnp.dot(
                    dx_ref[t], jnp.concatenate(parts, axis=0), preferred_element_type=F32
                )
            line = jnp.concatenate(
                [
                    vz[comp, pl.ds(3, cells), pl.ds(row, ROWS), c].reshape(size, -1)
                    for c in (pl.ds(before, 128), cols, pl.ds(after, 128))
                ],
                axis=1,
            )
            grad[3 * comp + 2] = jnp.dot(line, band_ref[...], preferred_element_type=F32)

        for h in range(WIDE // 128):
            to = b * (WIDE // 128) + h
            halves = []
            for r in range(ROWS // 8):
                cum = jnp.zeros((8, 128), F32)
                trans = jnp.ones((8, 128), F32)
                colour = [jnp.zeros((8, 128), F32) for _ in range(3)]
                for z in range(cells):
                    a = [grad[j, pl.ds(z * ROWS + 8 * r, 8), pl.ds(128 * h, 128)] for j in range(9)]
                    q = a[0] * a[0] + a[4] * a[4] + a[8] * a[8]
                    q = q + 2.0 * (a[1] * a[3] + a[2] * a[6] + a[5] * a[7])
                    place = jnp.tanh(q * Q_SCALE) * (0.5 * (KNOTS - 1)) + 0.5 * (KNOTS - 1)
                    index = place.astype(jnp.int32)
                    part = place - index.astype(F32)

                    def look(j, index=index):
                        return jnp.take_along_axis(tab[j], index, axis=1, mode="promise_in_bounds")

                    cum = cum + (look(6) + look(7) * part)
                    behind = jnp.exp2(cum)
                    weight = trans - behind
                    trans = behind
                    colour = [
                        colour[c] + (look(2 * c) + look(2 * c + 1) * part) * weight for c in range(3)
                    ]
                halves.append(colour + [trans])
            for c in range(4):
                full = jnp.concatenate([half[c] for half in halves], axis=0)
                high = full.astype(BF)
                packets[s, to, c] = high
                if c == 3:
                    packets[s, to, 4] = (full - high.astype(F32)).astype(BF)

            @pl.when(to == me)
            def _(to=to):
                a2a_own(s).start()

            @pl.when(to != me)
            def _(to=to):
                a2a_copy(s, to).start()

        return s

    def gather_copy(s, axis, i):
        return pltpu.make_async_remote_copy(
            src_ref=arrive.at[s, :, pl.ds(2 * axis, 2)],
            dst_ref=held.at[axis, s, pos[axis]],
            send_sem=s1_sem.at[s, axis, i - 1],
            recv_sem=r1_sem.at[s, axis, pos[axis]],
            device_id={"tile": peer(axis, i)[1]},
        )

    def gather_arrival(s, axis, i):
        place, to = peer(axis, i)
        return pltpu.make_async_remote_copy(
            src_ref=arrive.at[s, :, pl.ds(2 * axis, 2)],
            dst_ref=held.at[axis, s, place],
            send_sem=s1_sem.at[s, axis, i - 1],
            recv_sem=r1_sem.at[s, axis, place],
            device_id={"tile": to},
        )

    def pick_copy(s, axis, i):
        other = 1 - axis
        place, to = peer(other, i)
        return pltpu.make_async_remote_copy(
            src_ref=picked.at[axis, s, place],
            dst_ref=landed.at[axis, s, pos[other]],
            send_sem=s2_sem.at[s, axis, i - 1],
            recv_sem=r2_sem.at[s, axis, pos[other]],
            device_id={"tile": to},
        )

    def pick_arrival(s, axis, i):
        place, to = peer(1 - axis, i)
        return pltpu.make_async_remote_copy(
            src_ref=picked.at[axis, s, place],
            dst_ref=landed.at[axis, s, place],
            send_sem=s2_sem.at[s, axis, i - 1],
            recv_sem=r2_sem.at[s, axis, place],
            device_id={"tile": to},
        )

    def frame_step(s):
        rows = pl.ds(pl.multiple_of(lax.rem(s + 1, tiles) * ROWS, ROWS), ROWS)
        for i in range(1, n_depth):
            a2a_arrival(s, lax.rem(me + i, n_depth)).wait_recv()
        a2a_own(s).wait()
        for axis in (0, 1):
            for i in range(1, AXIS):
                gather_copy(s, axis, i).start()
        colour = [jnp.zeros((ROWS, 128), F32) for _ in range(3)]
        trans = jnp.ones((ROWS, 128), F32)
        for d in range(n_depth):
            image = [arrive[s, d, c] for c in range(5)]
            for axis in (0, 1):
                for c in (0, 1):
                    held[axis, s, pos[axis], d, c] = image[2 * axis + c]
            colour = [colour[c] + trans * image[c].astype(F32) for c in range(3)]
            trans = trans * (image[3].astype(F32) + image[4].astype(F32))
        for c in range(3):
            img_rgb[c, rows, :] = colour[c] + trans * colour[c]
        img_t[rows, :] = trans * trans

    def pick_step(s):
        @pl.when(s == 0)
        def _():
            for axis in (0, 1):
                for i in range(1, AXIS):
                    hot_arrival(axis, i).wait_recv()
            everything = pltpu.make_async_copy(hot_all, hot_here, hl_sem)
            everything.start()
            everything.wait()

        for axis in (0, 1):
            for i in range(1, AXIS):
                gather_arrival(s, axis, i).wait_recv()
            shelf[axis] = held[axis, s]
            for i in range(AXIS):
                place, _ = peer(1 - axis, i)
                for h in range(hot):
                    brick = hot_here[1 - axis, place, 0, h]
                    its_tile, slab = brick // n_depth, lax.rem(brick, n_depth)
                    its_place = its_tile // AXIS if axis == 0 else lax.rem(its_tile, AXIS)
                    image = shelf[axis, its_place, slab]
                    if i == 0:
                        landed[axis, s, place, h] = image
                    else:
                        picked[axis, s, place, h] = image
                if i > 0:
                    pick_copy(s, axis, i).start()

    def choose(axis, s, h, place):
        image = landed[axis, s, 0, h].astype(F32)
        for i in range(1, AXIS):
            image = jnp.where(place == i, landed[axis, s, i, h].astype(F32), image)
        return image

    def inset_step(s):
        rows = pl.ds(pl.multiple_of(lax.rem(s + 1, tiles) * ROWS, ROWS), ROWS)
        for axis in (0, 1):
            for i in range(1, AXIS):
                pick_arrival(s, axis, i).wait_recv()
        for h in range(hot):
            its_tile = hot_smem[0, h] // n_depth
            first = choose(0, s, h, lax.rem(its_tile, AXIS))
            last = choose(1, s, h, its_tile // AXIS)
            count = reps[0, h]
            trans = last[1]
            two = jnp.where(count >= 2, trans, 0.0)
            three = jnp.where(count >= 3, trans * trans, 0.0)
            total = 1.0 + two + three
            ins_rgb[0, h, 0, rows, :] = first[0] * total
            ins_rgb[0, h, 1, rows, :] = first[1] * total
            ins_rgb[0, h, 2, rows, :] = last[0] * total
            power = jnp.where(count >= 2, trans, 1.0) * trans
            ins_t[0, h, rows, :] = jnp.where(count >= 3, trans, 1.0) * power

    def step(k, carry):
        @pl.when(k < tiles)
        def _():
            z_copy(k, True).wait_recv()
            z_copy(k, False).wait_recv()

            @pl.when(k == tiles - 2)
            def _():
                x_copy(0).wait_recv()

            @pl.when(k == tiles - 1)
            def _():
                x_copy(1).wait_recv()

            lax.fori_loop(0, blocks, block_step, k)

        @pl.when((k >= 1) & (k < tiles + 1))
        def _():
            frame_step(k - 1)

        @pl.when((k >= 2) & (k < tiles + 2))
        def _():
            pick_step(k - 2)

        @pl.when(k >= 3)
        def _():
            inset_step(k - 3)

        return carry

    lax.fori_loop(0, tiles + 3, step, 0)

    for axis in (0, 1):
        for i in range(1, AXIS):
            hot_copy(axis, i).wait_send()
    x_copy(0).wait_send()
    x_copy(1).wait_send()

    def sent(s, carry):
        z_copy(s, True).wait_send()
        z_copy(s, False).wait_send()
        for i in range(1, n_depth):
            a2a_copy(s, lax.rem(me + i, n_depth)).wait_send()
        for axis in (0, 1):
            for i in range(1, AXIS):
                gather_copy(s, axis, i).wait_send()
                pick_copy(s, axis, i).wait_send()
        return carry

    lax.fori_loop(0, tiles, sent, 0)


def body(velocity, palette, bin_table, hot_ids, repeats):
    _, cells, width, length = velocity.shape
    n_depth, n_tile = lax.axis_size("depth"), lax.axis_size("tile")
    hot = hot_ids.shape[1]
    tiles = width // ROWS
    groups = 3 * cells // 4
    vmem, smem = pl.BlockSpec(memory_space=pltpu.VMEM), pl.BlockSpec(memory_space=pltpu.SMEM)
    dma, one = pltpu.SemaphoreType.DMA, pltpu.SemaphoreType.DMA
    constants = [
        jnp.asarray(m.astype(ml_dtypes.bfloat16))
        for m in (depth_matrix(cells), first_matrix(tiles), second_matrix(), pack_matrix())
    ]
    columns = length // n_depth
    return pl.pallas_call(
        functools.partial(render_kernel, (cells, width, length, n_depth, n_tile, hot)),
        out_shape=(
            jax.ShapeDtypeStruct((3, width, columns), F32),
            jax.ShapeDtypeStruct((width, columns), F32),
            jax.ShapeDtypeStruct((1, hot, 3, width, columns), F32),
            jax.ShapeDtypeStruct((1, hot, width, columns), F32),
        ),
        in_specs=[pl.BlockSpec(memory_space=pl.ANY), smem, smem, smem, vmem, smem] + [vmem] * 4,
        out_specs=(vmem, vmem, vmem, vmem),
        scratch_shapes=[
            pltpu.VMEM((3, cells + 6, width, length), BF),
            pltpu.VMEM((2, groups, ROWS, length), BF),
            pltpu.VMEM((3, groups, ROWS, length), BF),
            pltpu.VMEM((9, cells * ROWS, WIDE), F32),
            pltpu.VMEM((8, 8, 128), F32),
            pltpu.VMEM((tiles, n_depth, 5, ROWS, columns), BF),
            pltpu.VMEM((tiles, n_depth, 5, ROWS, columns), BF),
            pltpu.VMEM((2, tiles, AXIS, n_depth, 2, ROWS, columns), BF),
            pltpu.VMEM((2, AXIS, n_depth, 2, ROWS, columns), BF),
            pltpu.VMEM((2, tiles, AXIS, hot, 2, ROWS, columns), BF),
            pltpu.VMEM((2, tiles, AXIS, hot, 2, ROWS, columns), BF),
            pltpu.VMEM((2, AXIS, 1, hot), jnp.int32),
            pltpu.SMEM((2, AXIS, 1, hot), jnp.int32),
            dma((tiles,)),
            dma((tiles, 2)), dma((tiles, 2)),
            dma((2,)), dma((2,)),
            dma((2, AXIS)), dma((2, AXIS)), pltpu.SemaphoreType.DMA,
            dma((tiles, n_depth)), dma((tiles, n_depth)),
            dma((tiles, 2, AXIS)), dma((tiles, 2, AXIS)),
            dma((tiles, 2, AXIS)), dma((tiles, 2, AXIS)),
        ],
        compiler_params=pltpu.CompilerParams(
            collective_id=0, has_side_effects=True, vmem_limit_bytes=48 * 2**20
        ),
        cost_estimate=pl.CostEstimate(
            flops=3 * cells * width * length * 400, bytes_accessed=velocity.size * 2, transcendentals=0
        ),
        name="render",
    )(velocity, palette, bin_table, hot_ids, hot_ids, repeats, *constants)


def solution(mesh):
    placed = (P(None, "depth", "tile", None), P(), P(), P("tile", None), P("tile", None))
    return jax.shard_map(
        body,
        mesh=mesh,
        in_specs=placed,
        out_specs=(
            P(None, "tile", "depth"),
            P("tile", "depth"),
            P("tile", None, None, None, "depth"),
            P("tile", None, None, "depth"),
        ),
        check_vma=False,
    )
```

time: 382 us -> 68.3 us (0.18); the launches traced: 376 us -> 68 us
  other arithmetic: 146 us -> 0 us
  waiting for transfers between devices: 136 us -> 0 us
  local copies, waits for them, and re-layouts: 70.6 us -> 8.77 us
  Pallas kernels: 0 us -> 58.5 us
  between operations: 14.8 us -> 0.66 us
  starting transfers between devices: 8.52 us -> 0 us
    all_gather x2 -> x0, waiting for transfers between devices: 121 us -> none  [the longest x1 68.8 us: body(): every_brick = lax.all_gather(stored, 'tile', axis=0, tiled=True)]
    max x2 -> x0, other arithmetic: 86.5 us -> none  [shade(): weight = jnp.maximum(0.0, 1.0 - jnp.abs(position - knot))]
    pallas_call x0 -> x1, Pallas kernels: none -> 58.5 us  [body(): pl.pallas_call(functools.partial(render_kernel, (cells, width, length, n_...]
    slice x21 -> x0, local copies, waits for them, and re-layouts: 56.3 us -> none  [the longest x6 17.4 us: diff_roll(): first = jnp.roll(field, -1, axis) - jnp.roll(field, 1, axis)]
    add x10 -> x0, other arithmetic: 28.7 us -> none  [the longest x1 27.8 us: shade(): result = result + knot_vals[:, knot][:, None, None, None] * weight[None]]
    ppermute x4 -> x0, waiting for transfers between devices: 15.1 us -> none  [the longest x2 15.1 us: extended(): before = lax.ppermute(last, axis, up)]
    concatenate x11 -> x0, other arithmetic: 12 us -> none  [the longest x2 9.72 us: extended(): array = jnp.concatenate([before, array, after], axis=dim)]
    ppermute x4 -> x0, starting transfers between devices: 8.45 us -> none  [the longest x2 6.78 us: extended(): after = lax.ppermute(initial, axis, down)]
  transfers between devices with their start and end apart: 6 -> 0, of which waited for: 4 -> 0; matrix products, arithmetic and copies ran while one was open for 2% -> 0% of each run, Pallas kernels for 0% -> 0%
where the time goes in v1:
time: 68.3 us; the launch traced here: 68 us
  Pallas kernels  58.5 us (86%)
  local copies, waits for them, and re-layouts  8.77 us (13%)
    pallas_call x1, Pallas kernels, body(): pl.pallas_call(functools.partial(render_kernel, (cells, width, length, n_...  58.5 us
    unnamed x20, local copies, waits for them, and re-layouts  8.77 us

profile of v1, /device:TPU:0, one launch (start us, length us, event | category | flops | bytes accessed | tf_op | source)
XLA Modules:
  0.0 68.0 jit_solution(10026771126315686744)
XLA Ops:
  0.6 0.0 copy-start
  0.6 0.9 %copy-done = bf16[512,256]{1,0:T(8,128)(2,1)S(1)} copy-done((bf16[512,256]{1,0:T(8,128)(2,1)S(1)}, bf16[512,256]{1,0:T(8,128)(2,1)}, u32[]{:S(2)}) %copy-start) | copy-done | bytes 262168
  1.6 0.0 copy-start.1
  1.6 0.9 %copy-done.1 = bf16[256,352]{1,0:T(8,128)(2,1)S(1)} copy-done((bf16[256,352]{1,0:T(8,128)(2,1)S(1)}, bf16[256,352]{1,0:T(8,128)(2,1)}, u32[]{:S(2)}) %copy-start.1) | copy-done | bytes 180248
  2.5 0.0 copy-start.2
  2.5 0.9 %copy-done.2 = bf16[4,64,208]{2,1,0:T(8,128)(2,1)S(1)} copy-done((bf16[4,64,208]{2,1,0:T(8,128)(2,1)S(1)}, bf16[4,64,208]{2,1,0:T(8,128)(2,1)}, u32[]{:S(2)}) %copy-start.2) | copy-done | bytes 106520
  3.4 0.0 copy-start.3
  3.4 0.7 %copy-done.3 = bf16[2,16,64]{2,1,0:T(8,128)(2,1)S(1)} copy-done((bf16[2,16,64]{2,1,0:T(8,128)(2,1)S(1)}, bf16[2,16,64]{2,1,0:T(8,128)(2,1)}, u32[]{:S(2)}) %copy-start.3) | copy-done | bytes 4120
  4.1 0.0 copy-start.4
  4.1 0.7 copy-done.4
  4.8 0.0 copy-start.5
  4.8 0.7 copy-done.5
  5.5 0.0 copy-start.6
  5.5 0.7 copy-done.6
  6.1 0.0 copy-start.7
  6.1 0.7 copy-done.7
  6.8 58.5 %render.1 = (f32[3,64,128]{2,1,0:T(8,128)S(1)}, f32[64,128]{1,0:T(8,128)S(1)}, f32[1,4,3,64,128]{4,3,2,1,0:T(8,128)S(1)}, f32[1,4,64,128]{3,2,1,0:T(8,128)S(1)}) custom-call(bf16[3,16,64,1024]{3,2,1,0:T(8,128)(2,1)} %vel.1, f32[4,32]{1,0:T(4,128)S(1)} %copy-done.4, s32[17]{0:T(128)S(1)} %copy-done.6, s32[1,4]{1,0:T(1,128)S(1)} %copy-done.5, ...), custom_call_target="tpu_custom_call" | custom-call | flops 1258291200 | bytes 6291456 | tf_op jit(solution)/shard_map/render/pallas_call | solution.py:466
  65.3 0.6 copy.17
  66.0 0.6 copy.18
  66.6 0.7 %copy.19 = f32[1,4,3,64,128]{4,3,2,1,0:T(8,128)} copy(f32[1,4,3,64,128]{4,3,2,1,0:T(8,128)S(1)} %get-tuple-element.10) | data formatting | bytes 786432
  67.3 0.7 copy.20
Async XLA Ops:
  0.6 1.0 %copy-start = (bf16[512,256]{1,0:T(8,128)(2,1)S(1)}, bf16[512,256]{1,0:T(8,128)(2,1)}, u32[]{:S(2)}) copy-start(bf16[512,256]{1,0:T(8,128)(2,1)} %constant.10.clone.band_ref) | copy-start | bytes 786436
  1.6 0.9 %copy-start.1 = (bf16[256,352]{1,0:T(8,128)(2,1)S(1)}, bf16[256,352]{1,0:T(8,128)(2,1)}, u32[]{:S(2)}) copy-start(bf16[256,352]{1,0:T(8,128)(2,1)} %constant.8.clone.dz_ref) | copy-start | bytes 540676
  2.5 0.9 %copy-start.2 = (bf16[4,64,208]{2,1,0:T(8,128)(2,1)S(1)}, bf16[4,64,208]{2,1,0:T(8,128)(2,1)}, u32[]{:S(2)}) copy-start(bf16[4,64,208]{2,1,0:T(8,128)(2,1)} %constant.9.clone.dx_ref) | copy-start | bytes 319492
  3.4 0.7 %copy-start.3 = (bf16[2,16,64]{2,1,0:T(8,128)(2,1)S(1)}, bf16[2,16,64]{2,1,0:T(8,128)(2,1)}, u32[]{:S(2)}) copy-start(bf16[2,16,64]{2,1,0:T(8,128)(2,1)} %constant.11.clone.pack_ref) | copy-start | bytes 12292
  4.1 0.7 %copy-start.4 = (f32[4,32]{1,0:T(4,128)S(1)}, f32[4,32]{1,0:T(4,128)}, u32[]{:S(2)}) copy-start(f32[4,32]{1,0:T(4,128)} %palette.1) | copy-start | bytes 1540
  4.8 0.7 copy-start.5
  5.5 0.7 copy-start.6
  6.1 0.7 copy-start.7

commit v2 on v1

--- a/solution.py
+++ b/solution.py
@@ -14,6 +14,7 @@
 MAXREP = 3
 STENCIL = ((1, 45.0), (2, -9.0), (3, 1.0))
 TAPS = tuple((k, c) for k, c in STENCIL) + tuple((-k, -c) for k, c in STENCIL)
+HIGH, LOW = 32760.0, 32767.0
 Q_SCALE = -0.5 / 3600.0
 BF = jnp.bfloat16
 F32 = jnp.float32
@@ -67,10 +68,11 @@
 
 def render_kernel(
     sizes,
-    vel, palette, bins, hot_smem, hot_vmem, reps, dz_ref, dx_ref, band_ref, pack_ref,
+    vel, palette_in, bins_in, hot_in, reps_in, dz_in, dx_in, band_in, pack_in,
     img_rgb, img_t, ins_rgb, ins_t,
-    vz, xsend, xh, grad, tab, packets, arrive, held, shelf, picked, landed, hot_all, hot_here,
-    own_sem, zs_sem, zr_sem, xs_sem, xr_sem, hs_sem, hr_sem, hl_sem,
+    palette, bins, hot_smem, hot_vmem, reps, dz_ref, dx_ref, band_ref, pack_ref,
+    vz, xsend, xh, flat, deep_even, deep_odd, tab, unit, packets, arrive, held, shelf, picked, landed, hot_all, hot_here,
+    in_sem, own_sem, zs_sem, zr_sem, xs_sem, xr_sem, hs_sem, hr_sem, hl_sem,
     as_sem, ar_sem, s1_sem, r1_sem, s2_sem, r2_sem,
 ):
     cells, width, length, n_depth, n_tile, hot = sizes
@@ -89,14 +91,28 @@
     depth_up = lax.rem(me + 1, n_depth)
     depth_down = lax.rem(me + n_depth - 1, n_depth)
 
+    small = [
+        pltpu.make_async_copy(source, target, in_sem.at[n])
+        for n, (source, target) in enumerate(
+            (
+                (hot_in, hot_vmem), (pack_in, pack_ref), (palette_in, palette), (bins_in, bins),
+                (hot_in, hot_smem), (reps_in, reps), (dz_in, dz_ref), (dx_in, dx_ref), (band_in, band_ref),
+            )
+        )
+    ]
+
     def own_copy(t):
         rows = pl.ds(t * ROWS, ROWS)
         return pltpu.make_async_copy(
             vel.at[:, :, rows, :], vz.at[:, pl.ds(3, cells), rows, :], own_sem.at[t]
         )
 
-    for t in (0, 3, 1, 2):
-        own_copy(t).start()
+    own_copy(0).start()
+    own_copy(3).start()
+    for copy in small:
+        copy.start()
+    own_copy(1).start()
+    own_copy(2).start()
 
     barrier = pltpu.get_barrier_semaphore()
     for t in (tile_up, tile_down):
@@ -140,49 +156,58 @@
             device_id={"tile": to},
         )
 
+    small[0].wait()
     for axis in (0, 1):
         for i in range(1, AXIS):
             hot_copy(axis, i).start()
         hot_all[axis, pos[axis]] = hot_vmem[...]
 
+    def x_copy(side, comp):
+        groups = pl.ds(comp * (cells // 4), cells // 4)
+        return pltpu.make_async_remote_copy(
+            src_ref=xsend.at[side, groups],
+            dst_ref=xh.at[1 - side, groups],
+            send_sem=xs_sem.at[side, comp],
+            recv_sem=xr_sem.at[side, comp],
+            device_id={"tile": tile_up if side else tile_down},
+        )
+
     own_copy(0).wait()
     own_copy(3).wait()
-    for side in (0, 1):
-        rows = pl.ds((tiles - 1) * ROWS * side, ROWS)
-
-        def pack(g, carry, side=side, rows=rows):
-            planes = vz[g // (cells // 4), pl.ds(3 + 4 * lax.rem(g, cells // 4), 4), rows, :]
-            xsend[side, g] = jnp.dot(
-                pack_ref[side], planes.reshape(4 * ROWS, length), preferred_element_type=F32
-            ).astype(BF)
-            return carry
-
-        lax.fori_loop(0, 3 * cells // 4, pack, 0)
-
-    def x_copy(side):
-        return pltpu.make_async_remote_copy(
-            src_ref=xsend.at[side],
-            dst_ref=xh.at[1 - side],
-            send_sem=xs_sem.at[side],
-            recv_sem=xr_sem.at[side],
-            device_id={"tile": tile_up if side else tile_down},
-        )
-
-    x_copy(0).start()
-    x_copy(1).start()
+    small[1].wait()
+
+    def pack(comp, carry):
+        for side in (0, 1):
+            rows = pl.ds((tiles - 1) * ROWS * side, ROWS)
+            for quad in range(cells // 4):
+                planes = vz[comp, pl.ds(3 + 4 * quad, 4), rows, :]
+                xsend[side, comp * (cells // 4) + quad] = jnp.dot(
+                    pack_ref[side], planes.reshape(4 * ROWS, length), preferred_element_type=F32
+                ).astype(BF)
+            x_copy(side, comp).start()
+        return carry
+
+    lax.fori_loop(0, 3, pack, 0)
     xh[2] = jnp.zeros(xh.shape[1:], BF)
 
+    for copy in small[2:]:
+        copy.wait()
     lane = lax.broadcasted_iota(jnp.int32, (8, 128), 1)
     for c in range(4):
-        scale = -4.0 / (cells * n_depth) * math.log2(math.e) if c == 3 else 1.0
-        values = [palette[c, bins[k]] * scale for k in range(KNOTS)]
+        values = [palette[c, bins[k]] for k in range(KNOTS)]
         base = jnp.full((8, 128), values[KNOTS - 1], F32)
-        slope = jnp.zeros((8, 128), F32)
+        following = base
         for k in range(KNOTS - 1):
             base = jnp.where(lane == k, values[k], base)
-            slope = jnp.where(lane == k, values[k + 1] - values[k], slope)
-        tab[2 * c] = base
-        tab[2 * c + 1] = slope
+            following = jnp.where(lane == k, values[k + 1], following)
+        top = jnp.broadcast_to(jnp.max(base, axis=1, keepdims=True), (8, 128))
+        low = jnp.floor((following - base) / top * LOW + 0.5)
+        high = jnp.floor(base / top * HIGH - low * (1.0 / 65536.0) + 0.5)
+        tab[c] = high.astype(jnp.int32) * 65536 + low.astype(jnp.int32)
+        if c == 3:
+            unit[c] = top * (-4.0 / (cells * n_depth) * math.log2(math.e) / (HIGH * 65536.0))
+        else:
+            unit[c] = top * (1.0 / (HIGH * 65536.0))
 
     own_copy(1).wait()
     own_copy(2).wait()
@@ -208,7 +233,7 @@
     def a2a_own(s):
         return pltpu.make_async_copy(packets.at[s, me], arrive.at[s, me], ar_sem.at[s, me])
 
-    def block_step(b, s):
+    def first_second(b, s):
         t = lax.rem(s + 1, tiles)
         row = pl.multiple_of(t * ROWS, ROWS)
         above = pl.multiple_of(jnp.maximum(t - 1, 0) * ROWS, ROWS)
@@ -218,28 +243,34 @@
         before = pl.multiple_of(lax.rem(col + length - 128, length), 128)
         after = pl.multiple_of(lax.rem(col + WIDE, length), 128)
         cols = pl.ds(col, WIDE)
-        size = cells * ROWS
         for comp in range(3):
-            column = vz[comp, :, pl.ds(row, ROWS), cols].reshape((cells + 6) * ROWS, WIDE)
-            grad[3 * comp] = jnp.dot(dz_ref[...], column, preferred_element_type=F32)
             for quad in range(cells // 4):
                 zs = pl.ds(3 + 4 * quad, 4)
                 parts = [
                     vz[comp, zs, pl.ds(r, ROWS), cols].reshape(4 * ROWS, WIDE)
                     for r in (above, row, below)
                 ] + [xh[side, comp * (cells // 4) + quad, :, cols]]
-                grad[3 * comp + 1, pl.ds(quad * 4 * ROWS, 4 * ROWS)] = jnp.dot(
+                flat[b, 2 * comp, pl.ds(quad * 4 * ROWS, 4 * ROWS)] = jnp.dot(
                     dx_ref[t], jnp.concatenate(parts, axis=0), preferred_element_type=F32
                 )
             line = jnp.concatenate(
                 [
-                    vz[comp, pl.ds(3, cells), pl.ds(row, ROWS), c].reshape(size, -1)
+                    vz[comp, pl.ds(3, cells), pl.ds(row, ROWS), c].reshape(cells * ROWS, -1)
                     for c in (pl.ds(before, 128), cols, pl.ds(after, 128))
                 ],
                 axis=1,
             )
-            grad[3 * comp + 2] = jnp.dot(line, band_ref[...], preferred_element_type=F32)
-
+            flat[b, 2 * comp + 1] = jnp.dot(line, band_ref[...], preferred_element_type=F32)
+        return s
+
+    def depth_derivative(b, s, deep):
+        row = pl.multiple_of(lax.rem(s + 1, tiles) * ROWS, ROWS)
+        cols = pl.ds(pl.multiple_of(b * WIDE, WIDE), WIDE)
+        for comp in range(3):
+            column = vz[comp, :, pl.ds(row, ROWS), cols].reshape((cells + 6) * ROWS, WIDE)
+            deep[comp] = jnp.dot(dz_ref[...], column, preferred_element_type=F32)
+
+    def shade(b, s, deep):
         for h in range(WIDE // 128):
             to = b * (WIDE // 128) + h
             halves = []
@@ -248,24 +279,27 @@
                 trans = jnp.ones((8, 128), F32)
                 colour = [jnp.zeros((8, 128), F32) for _ in range(3)]
                 for z in range(cells):
-                    a = [grad[j, pl.ds(z * ROWS + 8 * r, 8), pl.ds(128 * h, 128)] for j in range(9)]
-                    q = a[0] * a[0] + a[4] * a[4] + a[8] * a[8]
-                    q = q + 2.0 * (a[1] * a[3] + a[2] * a[6] + a[5] * a[7])
+                    spot = (pl.ds(z * ROWS + 8 * r, 8), pl.ds(128 * h, 128))
+                    a = [
+                        [deep[j, spot[0], spot[1]]] + [flat[b, 2 * j + m, spot[0], spot[1]] for m in (0, 1)]
+                        for j in range(3)
+                    ]
+                    q = a[0][0] * a[0][0] + a[1][1] * a[1][1] + a[2][2] * a[2][2]
+                    q = q + 2.0 * (a[0][1] * a[1][0] + a[0][2] * a[2][0] + a[1][2] * a[2][1])
                     place = jnp.tanh(q * Q_SCALE) * (0.5 * (KNOTS - 1)) + 0.5 * (KNOTS - 1)
                     index = place.astype(jnp.int32)
-                    part = place - index.astype(F32)
-
-                    def look(j, index=index):
-                        return jnp.take_along_axis(tab[j], index, axis=1, mode="promise_in_bounds")
-
-                    cum = cum + (look(6) + look(7) * part)
-                    behind = jnp.exp2(cum)
+                    part = (place - index.astype(F32)) * (HIGH / LOW)
+
+                    def look(c, index=index, part=part):
+                        entry = jnp.take_along_axis(tab[c], index, axis=1, mode="promise_in_bounds")
+                        return entry.astype(F32) + (entry << 16).astype(F32) * part
+
+                    cum = cum + look(3)
+                    behind = jnp.exp2(cum * unit[3])
                     weight = trans - behind
                     trans = behind
-                    colour = [
-                        colour[c] + (look(2 * c) + look(2 * c + 1) * part) * weight for c in range(3)
-                    ]
-                halves.append(colour + [trans])
+                    colour = [colour[c] + look(c) * weight for c in range(3)]
+                halves.append([colour[c] * unit[c] for c in range(3)] + [trans])
             for c in range(4):
                 full = jnp.concatenate([half[c] for half in halves], axis=0)
                 high = full.astype(BF)
@@ -273,6 +307,10 @@
                 if c == 3:
                     packets[s, to, 4] = (full - high.astype(F32)).astype(BF)
 
+    def send(b, s):
+        for h in range(WIDE // 128):
+            to = b * (WIDE // 128) + h
+
             @pl.when(to == me)
             def _(to=to):
                 a2a_own(s).start()
@@ -281,6 +319,13 @@
             def _(to=to):
                 a2a_copy(s, to).start()
 
+    def two_blocks(j, s):
+        depth_derivative(2 * j + 1, s, deep_odd)
+        shade(2 * j, s, deep_even)
+        send(2 * j, s)
+        depth_derivative(jnp.minimum(2 * j + 2, blocks - 1), s, deep_even)
+        shade(2 * j + 1, s, deep_odd)
+        send(2 * j + 1, s)
         return s
 
     def gather_copy(s, axis, i):
@@ -398,21 +443,29 @@
             power = jnp.where(count >= 2, trans, 1.0) * trans
             ins_t[0, h, rows, :] = jnp.where(count >= 3, trans, 1.0) * power
 
+    lax.fori_loop(0, blocks, first_second, 0)
+
     def step(k, carry):
         @pl.when(k < tiles)
         def _():
             z_copy(k, True).wait_recv()
             z_copy(k, False).wait_recv()
-
-            @pl.when(k == tiles - 2)
-            def _():
-                x_copy(0).wait_recv()
-
-            @pl.when(k == tiles - 1)
-            def _():
-                x_copy(1).wait_recv()
-
-            lax.fori_loop(0, blocks, block_step, k)
+            depth_derivative(0, k, deep_even)
+            lax.fori_loop(0, blocks // 2, two_blocks, k)
+
+        @pl.when(k < tiles - 1)
+        def _():
+            for comp in range(3):
+
+                @pl.when(k == tiles - 3)
+                def _(comp=comp):
+                    x_copy(0, comp).wait_recv()
+
+                @pl.when(k == tiles - 2)
+                def _(comp=comp):
+                    x_copy(1, comp).wait_recv()
+
+            lax.fori_loop(0, blocks, first_second, k + 1)
 
         @pl.when((k >= 1) & (k < tiles + 1))
         def _():
@@ -433,8 +486,9 @@
     for axis in (0, 1):
         for i in range(1, AXIS):
             hot_copy(axis, i).wait_send()
-    x_copy(0).wait_send()
-    x_copy(1).wait_send()
+    for comp in range(3):
+        x_copy(0, comp).wait_send()
+        x_copy(1, comp).wait_send()
 
     def sent(s, carry):
         z_copy(s, True).wait_send()
@@ -456,13 +510,17 @@
     hot = hot_ids.shape[1]
     tiles = width // ROWS
     groups = 3 * cells // 4
-    vmem, smem = pl.BlockSpec(memory_space=pltpu.VMEM), pl.BlockSpec(memory_space=pltpu.SMEM)
-    dma, one = pltpu.SemaphoreType.DMA, pltpu.SemaphoreType.DMA
+    vmem, hbm = pl.BlockSpec(memory_space=pltpu.VMEM), pl.BlockSpec(memory_space=pltpu.HBM)
+    dma = pltpu.SemaphoreType.DMA
     constants = [
         jnp.asarray(m.astype(ml_dtypes.bfloat16))
         for m in (depth_matrix(cells), first_matrix(tiles), second_matrix(), pack_matrix())
     ]
     columns = length // n_depth
+    operands = [
+        pltpu.with_memory_space_constraint(x, pltpu.HBM)
+        for x in (velocity, palette, bin_table, hot_ids, repeats, *constants)
+    ]
     return pl.pallas_call(
         functools.partial(render_kernel, (cells, width, length, n_depth, n_tile, hot)),
         out_shape=(
@@ -471,14 +529,23 @@
             jax.ShapeDtypeStruct((1, hot, 3, width, columns), F32),
             jax.ShapeDtypeStruct((1, hot, width, columns), F32),
         ),
-        in_specs=[pl.BlockSpec(memory_space=pl.ANY), smem, smem, smem, vmem, smem] + [vmem] * 4,
+        in_specs=[hbm] * 9,
         out_specs=(vmem, vmem, vmem, vmem),
         scratch_shapes=[
+            pltpu.SMEM(palette.shape, F32),
+            pltpu.SMEM(bin_table.shape, jnp.int32),
+            pltpu.SMEM(hot_ids.shape, jnp.int32),
+            pltpu.VMEM(hot_ids.shape, jnp.int32),
+            pltpu.SMEM(repeats.shape, jnp.int32),
+            *[pltpu.VMEM(m.shape, BF) for m in constants],
             pltpu.VMEM((3, cells + 6, width, length), BF),
             pltpu.VMEM((2, groups, ROWS, length), BF),
             pltpu.VMEM((3, groups, ROWS, length), BF),
-            pltpu.VMEM((9, cells * ROWS, WIDE), F32),
-            pltpu.VMEM((8, 8, 128), F32),
+            pltpu.VMEM((length // WIDE, 6, cells * ROWS, WIDE), F32),
+            pltpu.VMEM((3, cells * ROWS, WIDE), F32),
+            pltpu.VMEM((3, cells * ROWS, WIDE), F32),
+            pltpu.VMEM((4, 8, 128), jnp.int32),
+            pltpu.VMEM((4, 8, 128), F32),
             pltpu.VMEM((tiles, n_depth, 5, ROWS, columns), BF),
             pltpu.VMEM((tiles, n_depth, 5, ROWS, columns), BF),
             pltpu.VMEM((2, tiles, AXIS, n_depth, 2, ROWS, columns), BF),
@@ -487,9 +554,9 @@
             pltpu.VMEM((2, tiles, AXIS, hot, 2, ROWS, columns), BF),
             pltpu.VMEM((2, AXIS, 1, hot), jnp.int32),
             pltpu.SMEM((2, AXIS, 1, hot), jnp.int32),
-            dma((tiles,)),
+            dma((9,)), dma((tiles,)),
             dma((tiles, 2)), dma((tiles, 2)),
-            dma((2,)), dma((2,)),
+            dma((2, 3)), dma((2, 3)),
             dma((2, AXIS)), dma((2, AXIS)), pltpu.SemaphoreType.DMA,
             dma((tiles, n_depth)), dma((tiles, n_depth)),
             dma((tiles, 2, AXIS)), dma((tiles, 2, AXIS)),
@@ -502,7 +569,7 @@
             flops=3 * cells * width * length * 400, bytes_accessed=velocity.size * 2, transcendentals=0
         ),
         name="render",
-    )(velocity, palette, bin_table, hot_ids, hot_ids, repeats, *constants)
+    )(*operands)
 
 
 def solution(mesh):

time: 68.3 us -> 56.2 us (0.82)
  local copies, waits for them, and re-layouts: 8.77 us -> 2.66 us
  Pallas kernels: 58.5 us -> 52.8 us
    unnamed x20 -> x4, local copies, waits for them, and re-layouts: 8.77 us -> 2.66 us
    pallas_call x1, Pallas kernels: 58.5 us -> 52.8 us  [body(): pl.pallas_call(functools.partial(render_kernel, (cells, width, length, n_...]
where the time goes in v2:
time: 56.2 us; the launch traced here: 56.1 us
  Pallas kernels  52.8 us (94%)
  local copies, waits for them, and re-layouts  2.66 us (5%)
  between operations  0.64 us (1%)
    pallas_call x1, Pallas kernels, body(): pl.pallas_call(functools.partial(render_kernel, (cells, width, length, n_...  52.8 us
    unnamed x4, local copies, waits for them, and re-layouts  2.66 us

profile of v2, /device:TPU:0, one launch (start us, length us, event | category | flops | bytes accessed | tf_op | source)
XLA Modules:
  0.0 56.1 jit_solution(17666987797922196740)
XLA Ops:
  0.6 52.8 %render.1 = (f32[3,64,128]{2,1,0:T(8,128)S(1)}, f32[64,128]{1,0:T(8,128)S(1)}, f32[1,4,3,64,128]{4,3,2,1,0:T(8,128)S(1)}, f32[1,4,64,128]{3,2,1,0:T(8,128)S(1)}) custom-call(bf16[3,16,64,1024]{3,2,1,0:T(8,128)(2,1)} %vel.1, f32[4,32]{1,0:T(4,128)} %palette_in.1, s32[17]{0:T(128)} %bins_in.1, s32[1,4]{1,0:T(1,128)} %hot_in.1, s32[1,4]{1,0:T(1,128)} %reps_in.1, ...), custom_call_target="tpu_custom_call" | custom-call | flops 1258291200 | bytes 6291456 | tf_op jit(solution)/shard_map/render/pallas_call | solution.py:524
  53.4 0.6 %copy.17 = f32[3,64,128]{2,1,0:T(8,128)} copy(f32[3,64,128]{2,1,0:T(8,128)S(1)} %get-tuple-element.8) | data formatting | bytes 196608
  54.1 0.6 %copy.18 = f32[64,128]{1,0:T(8,128)} copy(f32[64,128]{1,0:T(8,128)S(1)} %get-tuple-element.9) | data formatting | bytes 65536
  54.7 0.7 %copy.19 = f32[1,4,3,64,128]{4,3,2,1,0:T(8,128)} copy(f32[1,4,3,64,128]{4,3,2,1,0:T(8,128)S(1)} %get-tuple-element.10) | data formatting | bytes 786432
  55.4 0.7 %copy.20 = f32[1,4,64,128]{3,2,1,0:T(8,128)} copy(f32[1,4,64,128]{3,2,1,0:T(8,128)S(1)} %get-tuple-element.11) | data formatting | bytes 262144

commit v3 on v2

--- a/solution.py
+++ b/solution.py
@@ -14,7 +14,7 @@
 MAXREP = 3
 STENCIL = ((1, 45.0), (2, -9.0), (3, 1.0))
 TAPS = tuple((k, c) for k, c in STENCIL) + tuple((-k, -c) for k, c in STENCIL)
-HIGH, LOW = 32760.0, 32767.0
+HALF = 32760.0
 Q_SCALE = -0.5 / 3600.0
 BF = jnp.bfloat16
 F32 = jnp.float32
@@ -71,13 +71,14 @@
     vel, palette_in, bins_in, hot_in, reps_in, dz_in, dx_in, band_in, pack_in,
     img_rgb, img_t, ins_rgb, ins_t,
     palette, bins, hot_smem, hot_vmem, reps, dz_ref, dx_ref, band_ref, pack_ref,
-    vz, xsend, xh, flat, deep_even, deep_odd, tab, unit, packets, arrive, held, shelf, picked, landed, hot_all, hot_here,
+    vz, xsend, xh, flat_even, flat_odd, deep_even, deep_odd, tab, unit, packets, arrive, held, shelf, picked, landed, hot_all, hot_here,
     in_sem, own_sem, zs_sem, zr_sem, xs_sem, xr_sem, hs_sem, hr_sem, hl_sem,
     as_sem, ar_sem, s1_sem, r1_sem, s2_sem, r2_sem,
 ):
     cells, width, length, n_depth, n_tile, hot = sizes
     tiles = width // ROWS
     blocks = length // WIDE
+    flats = (flat_even, flat_odd)
     tile = lax.axis_index("tile")
     me = lax.axis_index("depth")
     pos = (tile // AXIS, lax.rem(tile, AXIS))
@@ -125,7 +126,7 @@
     pl.semaphore_wait(barrier, 2 + n_depth - 1 + 2 * (AXIS - 1))
 
     def z_copy(s, up):
-        rows = pl.ds(lax.rem(s + 1, tiles) * ROWS, ROWS)
+        rows = pl.ds((s + 1) % tiles * ROWS, ROWS)
         source, target = (cells - 3, 0) if up else (0, cells + 3)
         return pltpu.make_async_remote_copy(
             src_ref=vel.at[:, pl.ds(source, 3), rows, :],
@@ -135,7 +136,7 @@
             device_id={"depth": depth_up if up else depth_down},
         )
 
-    for s in range(tiles):
+    for s in range(3):
         for up in (True, False):
             z_copy(s, up).start()
 
@@ -188,7 +189,6 @@
         return carry
 
     lax.fori_loop(0, 3, pack, 0)
-    xh[2] = jnp.zeros(xh.shape[1:], BF)
 
     for copy in small[2:]:
         copy.wait()
@@ -201,13 +201,13 @@
             base = jnp.where(lane == k, values[k], base)
             following = jnp.where(lane == k, values[k + 1], following)
         top = jnp.broadcast_to(jnp.max(base, axis=1, keepdims=True), (8, 128))
-        low = jnp.floor((following - base) / top * LOW + 0.5)
-        high = jnp.floor(base / top * HIGH - low * (1.0 / 65536.0) + 0.5)
+        low = jnp.floor((following - base) / top * HALF + 0.5)
+        high = jnp.floor(base / top * HALF - low * (1.0 / 65536.0) + 0.5)
         tab[c] = high.astype(jnp.int32) * 65536 + low.astype(jnp.int32)
         if c == 3:
-            unit[c] = top * (-4.0 / (cells * n_depth) * math.log2(math.e) / (HIGH * 65536.0))
+            unit[c] = top * (-4.0 / (cells * n_depth) * math.log2(math.e) / (HALF * 65536.0))
         else:
-            unit[c] = top * (1.0 / (HIGH * 65536.0))
+            unit[c] = top * (1.0 / (HALF * 65536.0))
 
     own_copy(1).wait()
     own_copy(2).wait()
@@ -233,44 +233,52 @@
     def a2a_own(s):
         return pltpu.make_async_copy(packets.at[s, me], arrive.at[s, me], ar_sem.at[s, me])
 
-    def first_second(b, s):
-        t = lax.rem(s + 1, tiles)
-        row = pl.multiple_of(t * ROWS, ROWS)
-        above = pl.multiple_of(jnp.maximum(t - 1, 0) * ROWS, ROWS)
-        below = pl.multiple_of(jnp.minimum(t + 1, tiles - 1) * ROWS, ROWS)
-        side = jnp.where(t == 0, 0, jnp.where(t == tiles - 1, 1, 2))
+    def horizontal(b, s, first=True, second=True):
+        t = (s + 1) % tiles
+        flat = flats[s % 2]
+        rows = [pl.ds(r * ROWS, ROWS) for r in (max(t - 1, 0), t, min(t + 1, tiles - 1))]
+        side = {0: 0, tiles - 1: 1}.get(t)
         col = pl.multiple_of(b * WIDE, WIDE)
         before = pl.multiple_of(lax.rem(col + length - 128, length), 128)
         after = pl.multiple_of(lax.rem(col + WIDE, length), 128)
         cols = pl.ds(col, WIDE)
         for comp in range(3):
-            for quad in range(cells // 4):
+            for quad in range(cells // 4 if first else 0):
                 zs = pl.ds(3 + 4 * quad, 4)
-                parts = [
-                    vz[comp, zs, pl.ds(r, ROWS), cols].reshape(4 * ROWS, WIDE)
-                    for r in (above, row, below)
-                ] + [xh[side, comp * (cells // 4) + quad, :, cols]]
+                parts = [vz[comp, zs, r, cols].reshape(4 * ROWS, WIDE) for r in rows]
+                if side is not None:
+                    parts.append(xh[side, comp * (cells // 4) + quad, :, cols])
                 flat[b, 2 * comp, pl.ds(quad * 4 * ROWS, 4 * ROWS)] = jnp.dot(
-                    dx_ref[t], jnp.concatenate(parts, axis=0), preferred_element_type=F32
+                    dx_ref[t, :, : ROWS * (12 + (side is not None))],
+                    jnp.concatenate(parts, axis=0),
+                    preferred_element_type=F32,
                 )
-            line = jnp.concatenate(
-                [
-                    vz[comp, pl.ds(3, cells), pl.ds(row, ROWS), c].reshape(cells * ROWS, -1)
-                    for c in (pl.ds(before, 128), cols, pl.ds(after, 128))
-                ],
-                axis=1,
-            )
-            flat[b, 2 * comp + 1] = jnp.dot(line, band_ref[...], preferred_element_type=F32)
-        return s
+            if second:
+                line = jnp.concatenate(
+                    [
+                        vz[comp, pl.ds(3, cells), rows[1], c].reshape(cells * ROWS, -1)
+                        for c in (pl.ds(before, 128), cols, pl.ds(after, 128))
+                    ],
+                    axis=1,
+                )
+                flat[b, 2 * comp + 1] = jnp.dot(line, band_ref[...], preferred_element_type=F32)
+
+    def horizontal_loop(s, first=True, second=True):
+        def one(b, carry):
+            horizontal(b, s, first, second)
+            return carry
+
+        lax.fori_loop(0, blocks, one, 0)
 
     def depth_derivative(b, s, deep):
-        row = pl.multiple_of(lax.rem(s + 1, tiles) * ROWS, ROWS)
+        row = (s + 1) % tiles * ROWS
         cols = pl.ds(pl.multiple_of(b * WIDE, WIDE), WIDE)
         for comp in range(3):
             column = vz[comp, :, pl.ds(row, ROWS), cols].reshape((cells + 6) * ROWS, WIDE)
             deep[comp] = jnp.dot(dz_ref[...], column, preferred_element_type=F32)
 
     def shade(b, s, deep):
+        flat = flats[s % 2]
         for h in range(WIDE // 128):
             to = b * (WIDE // 128) + h
             halves = []
@@ -288,7 +296,7 @@
                     q = q + 2.0 * (a[0][1] * a[1][0] + a[0][2] * a[2][0] + a[1][2] * a[2][1])
                     place = jnp.tanh(q * Q_SCALE) * (0.5 * (KNOTS - 1)) + 0.5 * (KNOTS - 1)
                     index = place.astype(jnp.int32)
-                    part = (place - index.astype(F32)) * (HIGH / LOW)
+                    part = place - index.astype(F32)
 
                     def look(c, index=index, part=part):
                         entry = jnp.take_along_axis(tab[c], index, axis=1, mode="promise_in_bounds")
@@ -319,14 +327,30 @@
             def _(to=to):
                 a2a_copy(s, to).start()
 
-    def two_blocks(j, s):
-        depth_derivative(2 * j + 1, s, deep_odd)
-        shade(2 * j, s, deep_even)
-        send(2 * j, s)
-        depth_derivative(jnp.minimum(2 * j + 2, blocks - 1), s, deep_even)
-        shade(2 * j + 1, s, deep_odd)
-        send(2 * j + 1, s)
+    def chip_at(offset):
+        return lax.rem(me // 2 + offset, blocks)
+
+    def two_blocks(j, s, ahead):
+        even, odd = chip_at(2 + j), chip_at(1 - j)
+        depth_derivative(odd, s, deep_odd)
+        ahead(2 * j)
+        shade(even, s, deep_even)
+        send(even, s)
+        depth_derivative(chip_at(3), s, deep_even)
+        ahead(2 * j + 1)
+        shade(odd, s, deep_odd)
+        send(odd, s)
         return s
+
+    def render(s, ahead):
+        def loop(j, carry):
+            two_blocks(j, s, ahead)
+            return carry
+
+        z_copy(s, True).wait_recv()
+        z_copy(s, False).wait_recv()
+        depth_derivative(chip_at(2), s, deep_even)
+        lax.fori_loop(0, blocks // 2, loop, 0)
 
     def gather_copy(s, axis, i):
         return pltpu.make_async_remote_copy(
@@ -369,7 +393,7 @@
         )
 
     def frame_step(s):
-        rows = pl.ds(pl.multiple_of(lax.rem(s + 1, tiles) * ROWS, ROWS), ROWS)
+        rows = pl.ds((s + 1) % tiles * ROWS, ROWS)
         for i in range(1, n_depth):
             a2a_arrival(s, lax.rem(me + i, n_depth)).wait_recv()
         a2a_own(s).wait()
@@ -390,8 +414,7 @@
         img_t[rows, :] = trans * trans
 
     def pick_step(s):
-        @pl.when(s == 0)
-        def _():
+        if s == 0:
             for axis in (0, 1):
                 for i in range(1, AXIS):
                     hot_arrival(axis, i).wait_recv()
@@ -424,7 +447,7 @@
         return image
 
     def inset_step(s):
-        rows = pl.ds(pl.multiple_of(lax.rem(s + 1, tiles) * ROWS, ROWS), ROWS)
+        rows = pl.ds((s + 1) % tiles * ROWS, ROWS)
         for axis in (0, 1):
             for i in range(1, AXIS):
                 pick_arrival(s, axis, i).wait_recv()
@@ -443,45 +466,33 @@
             power = jnp.where(count >= 2, trans, 1.0) * trans
             ins_t[0, h, rows, :] = jnp.where(count >= 3, trans, 1.0) * power
 
-    lax.fori_loop(0, blocks, first_second, 0)
-
-    def step(k, carry):
-        @pl.when(k < tiles)
-        def _():
-            z_copy(k, True).wait_recv()
-            z_copy(k, False).wait_recv()
-            depth_derivative(0, k, deep_even)
-            lax.fori_loop(0, blocks // 2, two_blocks, k)
-
-        @pl.when(k < tiles - 1)
-        def _():
-            for comp in range(3):
-
-                @pl.when(k == tiles - 3)
-                def _(comp=comp):
-                    x_copy(0, comp).wait_recv()
-
-                @pl.when(k == tiles - 2)
-                def _(comp=comp):
-                    x_copy(1, comp).wait_recv()
-
-            lax.fori_loop(0, blocks, first_second, k + 1)
-
-        @pl.when((k >= 1) & (k < tiles + 1))
-        def _():
-            frame_step(k - 1)
-
-        @pl.when((k >= 2) & (k < tiles + 2))
-        def _():
-            pick_step(k - 2)
-
-        @pl.when(k >= 3)
-        def _():
-            inset_step(k - 3)
-
-        return carry
-
-    lax.fori_loop(0, tiles + 3, step, 0)
+    def nothing(b):
+        pass
+
+    horizontal_loop(0)
+    render(0, lambda b: horizontal(b, 1))
+    for up in (True, False):
+        z_copy(tiles - 1, up).start()
+    render(1, lambda b: horizontal(b, 2, first=False))
+    for comp in range(3):
+        x_copy(0, comp).wait_recv()
+    horizontal_loop(2, second=False)
+    frame_step(0)
+    for comp in range(3):
+        x_copy(1, comp).wait_recv()
+    render(2, lambda b: horizontal(b, 3))
+    frame_step(1)
+    pick_step(0)
+    render(3, nothing)
+    frame_step(2)
+    pick_step(1)
+    inset_step(0)
+    frame_step(3)
+    pick_step(2)
+    inset_step(1)
+    pick_step(3)
+    inset_step(2)
+    inset_step(3)
 
     for axis in (0, 1):
         for i in range(1, AXIS):
@@ -540,7 +551,8 @@
             *[pltpu.VMEM(m.shape, BF) for m in constants],
             pltpu.VMEM((3, cells + 6, width, length), BF),
             pltpu.VMEM((2, groups, ROWS, length), BF),
-            pltpu.VMEM((3, groups, ROWS, length), BF),
+            pltpu.VMEM((2, groups, ROWS, length), BF),
+            pltpu.VMEM((length // WIDE, 6, cells * ROWS, WIDE), F32),
             pltpu.VMEM((length // WIDE, 6, cells * ROWS, WIDE), F32),
             pltpu.VMEM((3, cells * ROWS, WIDE), F32),
             pltpu.VMEM((3, cells * ROWS, WIDE), F32),

time: 56.2 us -> 52.2 us (0.929)
  Pallas kernels: 52.8 us -> 48.8 us
    pallas_call x1, Pallas kernels: 52.8 us -> 48.8 us  [body(): pl.pallas_call(functools.partial(render_kernel, (cells, width, length, n_...]
where the time goes in v3:
time: 52.2 us; the launch traced here: 52.1 us
  Pallas kernels  48.8 us (93%)
  local copies, waits for them, and re-layouts  2.66 us (5%)
  between operations  0.64 us (1%)
    pallas_call x1, Pallas kernels, body(): pl.pallas_call(functools.partial(render_kernel, (cells, width, length, n_...  48.8 us
    unnamed x4, local copies, waits for them, and re-layouts  2.66 us

profile of v3, /device:TPU:0, one launch (start us, length us, event | category | flops | bytes accessed | tf_op | source)
XLA Modules:
  0.0 52.1 jit_solution(12160995325505906887)
XLA Ops:
  0.6 48.8 %render.1 = (f32[3,64,128]{2,1,0:T(8,128)S(1)}, f32[64,128]{1,0:T(8,128)S(1)}, f32[1,4,3,64,128]{4,3,2,1,0:T(8,128)S(1)}, f32[1,4,64,128]{3,2,1,0:T(8,128)S(1)}) custom-call(bf16[3,16,64,1024]{3,2,1,0:T(8,128)(2,1)} %vel.1, f32[4,32]{1,0:T(4,128)} %palette_in.1, s32[17]{0:T(128)} %bins_in.1, s32[1,4]{1,0:T(1,128)} %hot_in.1, s32[1,4]{1,0:T(1,128)} %reps_in.1, ...), custom_call_target="tpu_custom_call" | custom-call | flops 1258291200 | bytes 6291456 | tf_op jit(solution)/shard_map/render/pallas_call | solution.py:535
  49.4 0.6 %copy.17 = f32[3,64,128]{2,1,0:T(8,128)} copy(f32[3,64,128]{2,1,0:T(8,128)S(1)} %get-tuple-element.8) | data formatting | bytes 196608
  50.1 0.6 %copy.18 = f32[64,128]{1,0:T(8,128)} copy(f32[64,128]{1,0:T(8,128)S(1)} %get-tuple-element.9) | data formatting | bytes 65536
  50.7 0.7 %copy.19 = f32[1,4,3,64,128]{4,3,2,1,0:T(8,128)} copy(f32[1,4,3,64,128]{4,3,2,1,0:T(8,128)S(1)} %get-tuple-element.10) | data formatting | bytes 786432
  51.4 0.7 %copy.20 = f32[1,4,64,128]{3,2,1,0:T(8,128)} copy(f32[1,4,64,128]{3,2,1,0:T(8,128)S(1)} %get-tuple-element.11) | data formatting | bytes 262144

commit v4 on v3

--- a/solution.py
+++ b/solution.py
@@ -32,21 +32,21 @@
     return m
 
 
-def first_matrix(tiles):
-    m = np.zeros((tiles, 4 * ROWS, 13 * ROWS), np.float32)
-    for t in range(tiles):
-        for p in range(4):
-            for r in range(ROWS):
-                for k, c in TAPS:
-                    g = r + k
-                    if 0 <= g < ROWS:
-                        col = 4 * ROWS + p * ROWS + g
-                    elif g < 0:
-                        col = p * ROWS + ROWS + g if t > 0 else 12 * ROWS + 3 * p + 3 + g
-                    else:
-                        col = 8 * ROWS + p * ROWS + g - ROWS if t < tiles - 1 else 12 * ROWS + 3 * p + g - ROWS
-                    m[t, p * ROWS + r, col] = c
-    return m
+def first_matrices(cells):
+    inner = np.zeros((4 * ROWS, 12 * ROWS), np.float32)
+    edge = np.zeros((2, cells // 4, 4 * ROWS, 8 * ROWS + 3 * cells), np.float32)
+    for p in range(4):
+        for r in range(ROWS):
+            for k, c in TAPS:
+                g, row = r + k, p * ROWS + r
+                part = 1 + (g >= ROWS) - (g < 0)
+                spot = p * ROWS + g % ROWS
+                inner[row, part * 4 * ROWS + spot] = c
+                for quad in range(cells // 4):
+                    packed = 8 * ROWS + 3 * (4 * quad + p)
+                    edge[0, quad, row, packed + 3 + g if g < 0 else (part - 1) * 4 * ROWS + spot] = c
+                    edge[1, quad, row, packed + g - ROWS if g >= ROWS else part * 4 * ROWS + spot] = c
+    return inner, edge
 
 
 def second_matrix():
@@ -57,9 +57,9 @@
     return m
 
 
-def pack_matrix():
-    m = np.zeros((2, ROWS, 4 * ROWS), np.float32)
-    for p in range(4):
+def pack_matrix(cells):
+    m = np.zeros((2, 3 * cells, cells * ROWS), np.float32)
+    for p in range(cells):
         for r in range(3):
             m[0, 3 * p + r, p * ROWS + r] = 1.0
             m[1, 3 * p + r, p * ROWS + ROWS - 3 + r] = 1.0
@@ -68,9 +68,9 @@
 
 def render_kernel(
     sizes,
-    vel, palette_in, bins_in, hot_in, reps_in, dz_in, dx_in, band_in, pack_in,
+    vel, palette_in, bins_in, hot_in, reps_in, dz_in, inner_in, edge_in, band_in, pack_in,
     img_rgb, img_t, ins_rgb, ins_t,
-    palette, bins, hot_smem, hot_vmem, reps, dz_ref, dx_ref, band_ref, pack_ref,
+    palette, bins, hot_smem, hot_vmem, reps, dz_ref, inner_ref, edge_ref, band_ref, pack_ref,
     vz, xsend, xh, flat_even, flat_odd, deep_even, deep_odd, tab, unit, packets, arrive, held, shelf, picked, landed, hot_all, hot_here,
     in_sem, own_sem, zs_sem, zr_sem, xs_sem, xr_sem, hs_sem, hr_sem, hl_sem,
     as_sem, ar_sem, s1_sem, r1_sem, s2_sem, r2_sem,
@@ -97,7 +97,7 @@
         for n, (source, target) in enumerate(
             (
                 (hot_in, hot_vmem), (pack_in, pack_ref), (palette_in, palette), (bins_in, bins),
-                (hot_in, hot_smem), (reps_in, reps), (dz_in, dz_ref), (dx_in, dx_ref), (band_in, band_ref),
+                (hot_in, hot_smem), (reps_in, reps), (dz_in, dz_ref), (inner_in, inner_ref), (edge_in, edge_ref), (band_in, band_ref),
             )
         )
     ]
@@ -164,10 +164,9 @@
         hot_all[axis, pos[axis]] = hot_vmem[...]
 
     def x_copy(side, comp):
-        groups = pl.ds(comp * (cells // 4), cells // 4)
-        return pltpu.make_async_remote_copy(
-            src_ref=xsend.at[side, groups],
-            dst_ref=xh.at[1 - side, groups],
+        return pltpu.make_async_remote_copy(
+            src_ref=xsend.at[side, comp],
+            dst_ref=xh.at[1 - side, comp],
             send_sem=xs_sem.at[side, comp],
             recv_sem=xr_sem.at[side, comp],
             device_id={"tile": tile_up if side else tile_down},
@@ -180,11 +179,8 @@
     def pack(comp, carry):
         for side in (0, 1):
             rows = pl.ds((tiles - 1) * ROWS * side, ROWS)
-            for quad in range(cells // 4):
-                planes = vz[comp, pl.ds(3 + 4 * quad, 4), rows, :]
-                xsend[side, comp * (cells // 4) + quad] = jnp.dot(
-                    pack_ref[side], planes.reshape(4 * ROWS, length), preferred_element_type=F32
-                ).astype(BF)
+            planes = vz[comp, pl.ds(3, cells), rows, :].reshape(cells * ROWS, length)
+            xsend[side, comp] = jnp.dot(pack_ref[side], planes, preferred_element_type=F32).astype(BF)
             x_copy(side, comp).start()
         return carry
 
@@ -233,49 +229,54 @@
     def a2a_own(s):
         return pltpu.make_async_copy(packets.at[s, me], arrive.at[s, me], ar_sem.at[s, me])
 
-    def horizontal(b, s, first=True, second=True):
+    def horizontal(b, s):
         t = (s + 1) % tiles
         flat = flats[s % 2]
-        rows = [pl.ds(r * ROWS, ROWS) for r in (max(t - 1, 0), t, min(t + 1, tiles - 1))]
+        own = pl.ds(t * ROWS, ROWS)
         side = {0: 0, tiles - 1: 1}.get(t)
+        rows = [pl.ds(r * ROWS, ROWS) for r in (t - 1, t, t + 1) if 0 <= r < tiles]
         col = pl.multiple_of(b * WIDE, WIDE)
         before = pl.multiple_of(lax.rem(col + length - 128, length), 128)
         after = pl.multiple_of(lax.rem(col + WIDE, length), 128)
         cols = pl.ds(col, WIDE)
         for comp in range(3):
-            for quad in range(cells // 4 if first else 0):
+            for quad in range(cells // 4):
                 zs = pl.ds(3 + 4 * quad, 4)
                 parts = [vz[comp, zs, r, cols].reshape(4 * ROWS, WIDE) for r in rows]
                 if side is not None:
-                    parts.append(xh[side, comp * (cells // 4) + quad, :, cols])
+                    parts.append(xh[side, comp, :, cols])
                 flat[b, 2 * comp, pl.ds(quad * 4 * ROWS, 4 * ROWS)] = jnp.dot(
-                    dx_ref[t, :, : ROWS * (12 + (side is not None))],
+                    inner_ref[...] if side is None else edge_ref[side, quad],
                     jnp.concatenate(parts, axis=0),
                     preferred_element_type=F32,
                 )
-            if second:
-                line = jnp.concatenate(
-                    [
-                        vz[comp, pl.ds(3, cells), rows[1], c].reshape(cells * ROWS, -1)
-                        for c in (pl.ds(before, 128), cols, pl.ds(after, 128))
-                    ],
-                    axis=1,
-                )
-                flat[b, 2 * comp + 1] = jnp.dot(line, band_ref[...], preferred_element_type=F32)
-
-    def horizontal_loop(s, first=True, second=True):
+            line = jnp.concatenate(
+                [
+                    vz[comp, pl.ds(3, cells), own, c].reshape(cells * ROWS, -1)
+                    for c in (pl.ds(before, 128), cols, pl.ds(after, 128))
+                ],
+                axis=1,
+            )
+            flat[b, 2 * comp + 1] = jnp.dot(line, band_ref[...], preferred_element_type=F32)
+
+    def horizontal_loop(s):
         def one(b, carry):
-            horizontal(b, s, first, second)
+            horizontal(b, s)
             return carry
 
         lax.fori_loop(0, blocks, one, 0)
 
     def depth_derivative(b, s, deep):
+        size = cells // 2 * ROWS
         row = (s + 1) % tiles * ROWS
         cols = pl.ds(pl.multiple_of(b * WIDE, WIDE), WIDE)
         for comp in range(3):
             column = vz[comp, :, pl.ds(row, ROWS), cols].reshape((cells + 6) * ROWS, WIDE)
-            deep[comp] = jnp.dot(dz_ref[...], column, preferred_element_type=F32)
+            for half in (0, 1):
+                window = column[half * size : half * size + (cells // 2 + 6) * ROWS]
+                deep[comp, pl.ds(half * size, size)] = jnp.dot(
+                    dz_ref[...], window, preferred_element_type=F32
+                )
 
     def shade(b, s, deep):
         flat = flats[s % 2]
@@ -473,10 +474,9 @@
     render(0, lambda b: horizontal(b, 1))
     for up in (True, False):
         z_copy(tiles - 1, up).start()
-    render(1, lambda b: horizontal(b, 2, first=False))
     for comp in range(3):
         x_copy(0, comp).wait_recv()
-    horizontal_loop(2, second=False)
+    render(1, lambda b: horizontal(b, 2))
     frame_step(0)
     for comp in range(3):
         x_copy(1, comp).wait_recv()
@@ -520,12 +520,11 @@
     n_depth, n_tile = lax.axis_size("depth"), lax.axis_size("tile")
     hot = hot_ids.shape[1]
     tiles = width // ROWS
-    groups = 3 * cells // 4
     vmem, hbm = pl.BlockSpec(memory_space=pltpu.VMEM), pl.BlockSpec(memory_space=pltpu.HBM)
     dma = pltpu.SemaphoreType.DMA
     constants = [
         jnp.asarray(m.astype(ml_dtypes.bfloat16))
-        for m in (depth_matrix(cells), first_matrix(tiles), second_matrix(), pack_matrix())
+        for m in (depth_matrix(cells // 2), *first_matrices(cells), second_matrix(), pack_matrix(cells))
     ]
     columns = length // n_depth
     operands = [
@@ -540,7 +539,7 @@
             jax.ShapeDtypeStruct((1, hot, 3, width, columns), F32),
             jax.ShapeDtypeStruct((1, hot, width, columns), F32),
         ),
-        in_specs=[hbm] * 9,
+        in_specs=[hbm] * 10,
         out_specs=(vmem, vmem, vmem, vmem),
         scratch_shapes=[
             pltpu.SMEM(palette.shape, F32),
@@ -550,8 +549,8 @@
             pltpu.SMEM(repeats.shape, jnp.int32),
             *[pltpu.VMEM(m.shape, BF) for m in constants],
             pltpu.VMEM((3, cells + 6, width, length), BF),
-            pltpu.VMEM((2, groups, ROWS, length), BF),
-            pltpu.VMEM((2, groups, ROWS, length), BF),
+            pltpu.VMEM((2, 3, 3 * cells, length), BF),
+            pltpu.VMEM((2, 3, 3 * cells, length), BF),
             pltpu.VMEM((length // WIDE, 6, cells * ROWS, WIDE), F32),
             pltpu.VMEM((length // WIDE, 6, cells * ROWS, WIDE), F32),
             pltpu.VMEM((3, cells * ROWS, WIDE), F32),
@@ -566,7 +565,7 @@
             pltpu.VMEM((2, tiles, AXIS, hot, 2, ROWS, columns), BF),
             pltpu.VMEM((2, AXIS, 1, hot), jnp.int32),
             pltpu.SMEM((2, AXIS, 1, hot), jnp.int32),
-            dma((9,)), dma((tiles,)),
+            dma((10,)), dma((tiles,)),
             dma((tiles, 2)), dma((tiles, 2)),
             dma((2, 3)), dma((2, 3)),
             dma((2, AXIS)), dma((2, AXIS)), pltpu.SemaphoreType.DMA,

time: 52.2 us -> 51 us (0.977)
  Pallas kernels: 48.8 us -> 47.5 us
    pallas_call x1, Pallas kernels: 48.8 us -> 47.5 us  [body(): pl.pallas_call(functools.partial(render_kernel, (cells, width, length, n_...]
where the time goes in v4:
time: 51 us; the launch traced here: 50.8 us
  Pallas kernels  47.5 us (93%)
  local copies, waits for them, and re-layouts  2.66 us (5%)
  between operations  0.64 us (1%)
    pallas_call x1, Pallas kernels, body(): pl.pallas_call(functools.partial(render_kernel, (cells, width, length, n_...  47.5 us
    unnamed x4, local copies, waits for them, and re-layouts  2.66 us

profile of v4, /device:TPU:0, one launch (start us, length us, event | category | flops | bytes accessed | tf_op | source)
XLA Modules:
  0.0 50.8 jit_solution(3854479713054593525)
XLA Ops:
  0.6 47.5 %render.1 = (f32[3,64,128]{2,1,0:T(8,128)S(1)}, f32[64,128]{1,0:T(8,128)S(1)}, f32[1,4,3,64,128]{4,3,2,1,0:T(8,128)S(1)}, f32[1,4,64,128]{3,2,1,0:T(8,128)S(1)}) custom-call(bf16[3,16,64,1024]{3,2,1,0:T(8,128)(2,1)} %vel.1, f32[4,32]{1,0:T(4,128)} %palette_in.1, s32[17]{0:T(128)} %bins_in.1, s32[1,4]{1,0:T(1,128)} %hot_in.1, s32[1,4]{1,0:T(1,128)} %reps_in.1, ...), custom_call_target="tpu_custom_call" | custom-call | flops 1258291200 | bytes 6291456 | tf_op jit(solution)/shard_map/render/pallas_call | solution.py:534
  48.1 0.6 %copy.18 = f32[3,64,128]{2,1,0:T(8,128)} copy(f32[3,64,128]{2,1,0:T(8,128)S(1)} %get-tuple-element.8) | data formatting | bytes 196608
  48.8 0.6 %copy.19 = f32[64,128]{1,0:T(8,128)} copy(f32[64,128]{1,0:T(8,128)S(1)} %get-tuple-element.9) | data formatting | bytes 65536
  49.4 0.7 %copy.20 = f32[1,4,3,64,128]{4,3,2,1,0:T(8,128)} copy(f32[1,4,3,64,128]{4,3,2,1,0:T(8,128)S(1)} %get-tuple-element.10) | data formatting | bytes 786432
  50.2 0.7 %copy.21 = f32[1,4,64,128]{3,2,1,0:T(8,128)} copy(f32[1,4,64,128]{3,2,1,0:T(8,128)S(1)} %get-tuple-element.11) | data formatting | bytes 262144

commit v5 on v4

--- a/solution.py
+++ b/solution.py
@@ -427,12 +427,12 @@
             for i in range(1, AXIS):
                 gather_arrival(s, axis, i).wait_recv()
             shelf[axis] = held[axis, s]
-            for i in range(AXIS):
+            for i in (1, 2, 3, 0):
                 place, _ = peer(1 - axis, i)
                 for h in range(hot):
                     brick = hot_here[1 - axis, place, 0, h]
-                    its_tile, slab = brick // n_depth, lax.rem(brick, n_depth)
-                    its_place = its_tile // AXIS if axis == 0 else lax.rem(its_tile, AXIS)
+                    its_tile, slab = lax.div(brick, n_depth), lax.rem(brick, n_depth)
+                    its_place = lax.div(its_tile, AXIS) if axis == 0 else lax.rem(its_tile, AXIS)
                     image = shelf[axis, its_place, slab]
                     if i == 0:
                         landed[axis, s, place, h] = image
@@ -490,9 +490,6 @@
     frame_step(3)
     pick_step(2)
     inset_step(1)
-    pick_step(3)
-    inset_step(2)
-    inset_step(3)
 
     for axis in (0, 1):
         for i in range(1, AXIS):
@@ -501,18 +498,27 @@
         x_copy(0, comp).wait_send()
         x_copy(1, comp).wait_send()
 
-    def sent(s, carry):
+    def images_sent(s, carry):
         z_copy(s, True).wait_send()
         z_copy(s, False).wait_send()
         for i in range(1, n_depth):
             a2a_copy(s, lax.rem(me + i, n_depth)).wait_send()
+        return carry
+
+    def bricks_sent(s, carry):
         for axis in (0, 1):
             for i in range(1, AXIS):
                 gather_copy(s, axis, i).wait_send()
                 pick_copy(s, axis, i).wait_send()
         return carry
 
-    lax.fori_loop(0, tiles, sent, 0)
+    lax.fori_loop(0, tiles, images_sent, 0)
+    lax.fori_loop(0, tiles - 2, bricks_sent, 0)
+    pick_step(3)
+    inset_step(2)
+    bricks_sent(tiles - 2, 0)
+    inset_step(3)
+    bricks_sent(tiles - 1, 0)
 
 
 def body(velocity, palette, bin_table, hot_ids, repeats):

time: 51 us -> 50.6 us (level)
  no operation moved by 1% of the time
where the time goes in v5:
time: 50.6 us; the launch traced here: 50.4 us
  Pallas kernels  47.1 us (93%)
  local copies, waits for them, and re-layouts  2.66 us (5%)
  between operations  0.64 us (1%)
    pallas_call x1, Pallas kernels, body(): pl.pallas_call(functools.partial(render_kernel, (cells, width, length, n_...  47.1 us
    unnamed x4, local copies, waits for them, and re-layouts  2.66 us

profile of v5, /device:TPU:0, one launch (start us, length us, event | category | flops | bytes accessed | tf_op | source)
XLA Modules:
  0.0 50.4 jit_solution(10372692474005360923)
XLA Ops:
  0.6 47.1 %render.1 = (f32[3,64,128]{2,1,0:T(8,128)S(1)}, f32[64,128]{1,0:T(8,128)S(1)}, f32[1,4,3,64,128]{4,3,2,1,0:T(8,128)S(1)}, f32[1,4,64,128]{3,2,1,0:T(8,128)S(1)}) custom-call(bf16[3,16,64,1024]{3,2,1,0:T(8,128)(2,1)} %vel.1, f32[4,32]{1,0:T(4,128)} %palette_in.1, s32[17]{0:T(128)} %bins_in.1, s32[1,4]{1,0:T(1,128)} %hot_in.1, s32[1,4]{1,0:T(1,128)} %reps_in.1, ...), custom_call_target="tpu_custom_call" | custom-call | flops 1258291200 | bytes 6291456 | tf_op jit(solution)/shard_map/render/pallas_call | solution.py:540
  47.7 0.6 %copy.18 = f32[3,64,128]{2,1,0:T(8,128)} copy(f32[3,64,128]{2,1,0:T(8,128)S(1)} %get-tuple-element.8) | data formatting | bytes 196608
  48.4 0.6 %copy.19 = f32[64,128]{1,0:T(8,128)} copy(f32[64,128]{1,0:T(8,128)S(1)} %get-tuple-element.9) | data formatting | bytes 65536
  49.0 0.7 %copy.20 = f32[1,4,3,64,128]{4,3,2,1,0:T(8,128)} copy(f32[1,4,3,64,128]{4,3,2,1,0:T(8,128)S(1)} %get-tuple-element.10) | data formatting | bytes 786432
  49.7 0.7 %copy.21 = f32[1,4,64,128]{3,2,1,0:T(8,128)} copy(f32[1,4,64,128]{3,2,1,0:T(8,128)S(1)} %get-tuple-element.11) | data formatting | bytes 262144
